TPU v7x, 128 devices: a whole 4x4x4 slice. The times are simulated.
128 devices in a mesh: dp: 8 (over z_lo, x), fsdp: 16 (over y, z_hi, core).
Axes of the slice: x: 4, y: 4, z: 4 (z_hi: 2, z_lo: 2; z = z_hi * 2 + z_lo), core: 2. Of those that a mesh axis runs over, the one named last changes fastest.
Arguments:
- queries: bfloat16 [65536, 2048], P(('dp', 'fsdp')), may hold values from -6 to 6
- keys: bfloat16 [65536, 2048], P(('dp', 'fsdp')), may hold values from -6 to 6
- values: bfloat16 [65536, 2048], P(('dp', 'fsdp')), may hold values from -6 to 6
- attn_out: bfloat16 [65536, 2048], P(('dp', 'fsdp')), may hold values from -24 to 24
- out_grad: bfloat16 [65536, 2048], P(('dp', 'fsdp')), may hold values from -6 to 6
- log_norm: float32 [65536, 16], P(('dp', 'fsdp')), may hold values from 4 to 7
- segment_ids: int32 [128, 4], P(('dp', 'fsdp')), may hold values from 0 to 3, as said below
- kept_tokens: int32 [128, 4], P(('dp', 'fsdp')), may hold values from 0 to 512, as said below
- out_weight: bfloat16 [2048, 2048], P('fsdp'), may hold values from -0.125 to 0.125
Outputs:
- query_grad: bfloat16 [65536, 2048], P(('dp', 'fsdp'))
- key_grad: bfloat16 [65536, 2048], P(('dp', 'fsdp'))
- value_grad: bfloat16 [65536, 2048], P(('dp', 'fsdp'))
- weight_grad: float32 [2048, 2048], P('fsdp')
Inputs may be any that keep to these rules, and one draw needn't show every extreme that they name: `segment_ids`: row p numbers the images of pack p block by block: 0 for block 0, rising by one at each block that starts a new image. Some pack is one image, some pack has one image a block. `kept_tokens`: entry (p, i) counts the kept tokens of image i of pack p, which fill the start of that image's blocks: an image of b blocks keeps 128 (b - 1) + 1 to 128 b tokens; numbers with no image hold 0.
All inputs are finite; a program needn't handle non-finite values.
Results may differ from a plain program's by a relative error of at most 0.012.
The roundings to bfloat16 on the way count: a program that leaves them out, or rounds other values in their place, can miss the bound.
Values may be sent and summed in bfloat16 or wider, within the bound.
A program may use at most 192 MiB of HBM per device.

v0:
```python
import jax
import jax.numpy as jnp
from jax import lax
from jax.sharding import PartitionSpec as P

BLOCK = 128


def pair_grads(query_heads, key_heads, value_heads, grad_heads, norm_rows, delta_rows, key_live):
    score_scale = query_heads.shape[2] ** (-0.5)
    scores = (
        jnp.einsum("hqd,hkd->hqk", query_heads, key_heads, preferred_element_type=jnp.float32)
        * score_scale
    )
    probs = jnp.where(key_live[None, None, :], jnp.exp(scores - norm_rows[:, :, None]), 0.0)
    value_grad = jnp.einsum(
        "hqk,hqd->hkd", probs.astype(jnp.bfloat16), grad_heads, preferred_element_type=jnp.float32
    )
    prob_grad = jnp.einsum(
        "hqd,hkd->hqk", grad_heads, value_heads, preferred_element_type=jnp.float32
    )
    score_grad = (probs * (prob_grad - delta_rows[:, :, None])).astype(jnp.bfloat16)
    query_grad = (
        jnp.einsum("hqk,hkd->hqd", score_grad, key_heads, preferred_element_type=jnp.float32)
        * score_scale
    )
    key_grad = (
        jnp.einsum("hqk,hqd->hkd", score_grad, query_heads, preferred_element_type=jnp.float32)
        * score_scale
    )
    return (query_grad, key_grad, value_grad)


def to_blocks(rows, block_count, head_count):
    return rows.reshape(block_count, BLOCK, head_count, rows.shape[1] // head_count).transpose(
        0, 2, 1, 3
    )


def from_blocks(blocked):
    block_count, head_count, block_rows, head_size = blocked.shape
    return (
        blocked.transpose(0, 2, 1, 3)
        .reshape(block_count * block_rows, head_count * head_size)
        .astype(jnp.bfloat16)
    )


def per_device(
    queries, keys, values, attn_out, out_grad, log_norm, segment_ids, kept_tokens, out_weight
):
    tok_rows = queries.shape[0]
    feat_width = queries.shape[1]
    head_count = log_norm.shape[1]
    head_size = feat_width // head_count
    block_count = tok_rows // BLOCK
    seg_ids = segment_ids[0]
    kept_counts = kept_tokens[0]
    block_ids = jnp.arange(block_count)
    first_block = jnp.sum((seg_ids[None, :] < seg_ids[:, None]).astype(jnp.int32), axis=1)
    block_kept = jnp.sum(
        (seg_ids[:, None] == block_ids[None, :]).astype(jnp.int32) * kept_counts[None, :], axis=1
    )
    positions = (block_ids - first_block)[:, None] * BLOCK + jnp.arange(BLOCK)[None, :]
    block_valid = positions < block_kept[:, None]
    token_valid = block_valid.reshape(tok_rows)
    grad_input = jnp.where(token_valid[:, None], out_grad, jnp.zeros_like(out_grad))
    attn_grad = lax.dot_general(
        grad_input,
        lax.all_gather(out_weight, "fsdp", axis=0, tiled=True),
        (((1,), (1,)), ((), ())),
        preferred_element_type=jnp.float32,
    ).astype(jnp.bfloat16)
    delta = jnp.sum(
        (attn_grad.astype(jnp.float32) * attn_out.astype(jnp.float32)).reshape(
            tok_rows, head_count, head_size
        ),
        axis=2,
    )
    grad_share = lax.psum_scatter(
        lax.dot_general(
            attn_out, grad_input, (((0,), (0,)), ((), ())), preferred_element_type=jnp.float32
        ),
        "fsdp",
        scatter_dimension=0,
        tiled=True,
    )
    weight_grad = lax.psum(grad_share, "dp")
    query_blocks = to_blocks(queries, block_count, head_count)
    key_blocks = to_blocks(keys, block_count, head_count)
    value_blocks = to_blocks(values, block_count, head_count)
    grad_blocks = to_blocks(attn_grad, block_count, head_count)
    norm_blocks = log_norm.reshape(block_count, BLOCK, head_count).transpose(0, 2, 1)
    delta_blocks = delta.reshape(block_count, BLOCK, head_count).transpose(0, 2, 1)
    pair_ids = jnp.arange(block_count * block_count)
    pair_live = (seg_ids[pair_ids // block_count] == seg_ids[pair_ids % block_count]).astype(
        jnp.int32
    )
    pair_order = jnp.argsort(1 - pair_live, stable=True)
    pair_total = jnp.sum(pair_live)

    def take_blocks(query_block, key_block):
        return (
            query_blocks[query_block],
            key_blocks[key_block],
            value_blocks[key_block],
            grad_blocks[query_block],
            norm_blocks[query_block],
            delta_blocks[query_block],
            block_valid[key_block],
        )

    def run_pair(pair_step, totals):
        pair_index = pair_order[pair_step]
        query_block = pair_index // block_count
        key_block = pair_index % block_count
        query_term, key_term, value_term = pair_grads(*take_blocks(query_block, key_block))
        return (
            totals[0].at[query_block].add(query_term),
            totals[1].at[key_block].add(key_term),
            totals[2].at[key_block].add(value_term),
        )

    empty = jnp.zeros((block_count, head_count, BLOCK, head_size), jnp.float32)
    totals = (empty, empty, empty)
    totals = lax.fori_loop(0, pair_total, run_pair, totals)
    return (from_blocks(totals[0]), from_blocks(totals[1]), from_blocks(totals[2]), weight_grad)


def solution(mesh):
    placed = (
        P(("dp", "fsdp"), None),
        P(("dp", "fsdp"), None),
        P(("dp", "fsdp"), None),
        P(("dp", "fsdp"), None),
        P(("dp", "fsdp"), None),
        P(("dp", "fsdp"), None),
        P(("dp", "fsdp"), None),
        P(("dp", "fsdp"), None),
        P("fsdp", None),
    )
    return jax.shard_map(
        per_device,
        mesh=mesh,
        in_specs=placed,
        out_specs=(
            P(("dp", "fsdp"), None),
            P(("dp", "fsdp"), None),
            P(("dp", "fsdp"), None),
            P("fsdp", None),
        ),
        check_vma=False,
    )
```

profile of v0, /device:TPU:0, one launch (start us, length us, event | category | flops | bytes accessed | tf_op | source)
XLA Modules:
  0.0 482.2 jit_solution(11948150179926760325)
XLA Ops:
  9.0 12.6 %convolution_bitcast_fusion.1 = f32[2048,2048]{0,1:T(8,128)} fusion(bf16[512,2048]{1,0:T(8,128)(2,1)} %param.20, bf16[512,2048]{1,0:T(8,128)(2,1)} %param.21, pred[512]{0:T(512)(128)(4,1)S(1)} %fusion.27), kind=kOutput, calls=%fused_computation.45 | convolution fusion | flops 4296015872 | bytes 20972032 | tf_op jit(solution)/shard_map/dot_general | solution.py:81
  37.7 48.0 %all-gather.2.cloned.1.call-done = bf16[2048,2048]{1,0:T(8,128)(2,1)} async-done(((bf16[128,2048]{1,0:T(8,128)(2,1)}), bf16[2048,2048]{1,0:T(8,128)(2,1)}) %all-gather.2.cloned.1.call-update) | async-done | bytes 8388624 | tf_op jit(solution)/shard_map/all_gather | solution.py:70
  85.7 8.4 %convolution_convert_fusion = bf16[512,2048]{1,0:T(8,128)(2,1)S(1)} fusion(bf16[2048,2048]{1,0:T(8,128)(2,1)} %all-gather.2.cloned.1.call-done, bf16[512,2048]{1,0:T(8,128)(2,1)S(1)} %copy-done.10, pred[512]{0:T(512)(128)(4,1)S(1)} %fusion.27), kind=kOutput, calls=%fused_computation.47 | convolution fusion | flops 4297064448 | bytes 12583424 | tf_op jit(solution)/shard_map/dot_general | solution.py:68
  100.6 4.1 reduce_sum.39
  113.1 286.7 %while.19 = (s32[]{:T(128)}, f32[4,16,128,128]{3,2,1,0:T(8,128)}, f32[4,16,128,128]{3,2,1,0:T(8,128)}, f32[4,16,128,128]{3,2,1,0:T(8,128)}, s32[]{:T(128)}, /*in...) while((s32[]{:T(128)}, f32[4,16,128,128]{3,2,1,0:T(8,128)}, ...), condition=%wide.region_8.9_spmd, body=%wide.region_5.8_spmd.sunk | while | flops 339476544 | bytes 17879468 | solution.py:126
  121.6 3.3 fusion.49
  124.9 3.2 fusion.47
  128.1 3.5 fusion.48
  139.8 3.2 fusion.49
  143.0 3.2 fusion.47
  146.2 3.3 fusion.48
  157.7 3.2 fusion.49
  161.0 3.2 fusion.47
  164.2 3.2 fusion.48
  175.6 3.2 fusion.49
  178.8 3.2 fusion.47
  182.0 3.2 fusion.48
  193.4 3.3 fusion.49
  196.7 3.3 fusion.47
  200.0 3.2 fusion.48
  211.5 3.2 fusion.49
  214.7 3.3 fusion.47
  217.9 3.3 fusion.48
  229.4 3.2 fusion.49
  232.6 3.2 fusion.47
  235.8 3.2 fusion.48
  247.2 3.2 fusion.49
  250.4 3.2 fusion.47
  253.7 3.2 fusion.48
  265.0 3.3 fusion.49
  268.3 3.2 fusion.47
  271.5 3.2 fusion.48
  282.9 3.2 fusion.49
  289.3 3.2 fusion.48
  300.7 3.2 fusion.49
  303.9 3.2 fusion.47
  307.1 3.2 fusion.48
  318.5 3.2 fusion.49
  321.7 3.2 fusion.47
  324.9 3.2 fusion.48
  336.2 3.3 fusion.49
  342.7 3.2 fusion.48
  354.1 3.2 fusion.49
  360.5 3.2 fusion.48
  371.9 3.2 fusion.49
  378.3 3.2 fusion.48
  396.0 3.2 fusion.48
  415.2 58.0 %all-reduce.2.cloned.1.call-done = f32[128,2048]{0,1:T(8,128)} async-done(((f32[128,2048]{0,1:T(8,128)}), f32[128,2048]{0,1:T(8,128)}) %all-reduce.2.cloned.1.call-update) | async-done | bytes 1048592 | tf_op jit(solution)/shard_map/psum | solution.py:88
  (200 shorter events, 148.6 us)
Async XLA Ops:
  7.2 78.5 %all-gather.2.cloned.1.call-start = ((), (), s32[]{:S(2)}) async-start(), calls=%async_computation.1 | async-start | bytes 8912896 | tf_op jit(solution)/shard_map/all_gather | solution.py:70
  7.9 392.0 %reduce-scatter.2.cloned.1.call-start = ((), (), s32[]{:S(2)}) async-start(), calls=%async_computation.2 | async-start | bytes 17825792 | tf_op jit(solution)/shard_map/reduce_scatter | solution.py:80
  21.6 0.7 copy-start
  21.6 2.0 copy-start.8
  21.6 451.6 %all-reduce.2.cloned.1.call-start = ((), (), s32[]{:S(2)}) async-start(), calls=%async_computation.3 | async-start | bytes 2097152 | tf_op jit(solution)/shard_map/psum | solution.py:88
  23.6 2.4 copy-start.5
  26.0 2.0 copy-start.6
  31.9 2.2 copy-start.3
  31.9 3.0 copy-start.4
  35.0 50.8 %copy-start.10 = (bf16[512,2048]{1,0:T(8,128)(2,1)S(1)}, bf16[512,2048]{1,0:T(8,128)(2,1)}, u32[]{:S(2)}) copy-start(bf16[512,2048]{1,0:T(8,128)(2,1)} %param.21) | copy-start | bytes 6291460
  94.7 2.0 copy-start.7
  110.4 2.8 copy-start.9
  403.9 3.0 copy-start.2
  408.6 3.0 copy-start.1
Sparse Core Ops, SparseCore 0:
  10.4 75.2 all-gather.1
  90.1 144.9 reduce-scatter.1
  400.0 73.0 all-reduce.1
where the time goes:
time: 487 us; the launch traced here: 482 us
  matrix products  192 us (39%)
  waiting for transfers between devices  107 us (22%)
  local copies, waits for them, and re-layouts  92.4 us (19%)
  loops' own time  53.1 us (11%)
  other arithmetic  23.7 us (5%)
  between operations  14 us (3%)
    psum x1, waiting for transfers between devices, per_device(): weight_grad = lax.psum(grad_share, 'dp')  58 us
    another operation x1, loops' own time, per_device(): totals = lax.fori_loop(0, pair_total, run_pair, totals)  53.1 us
    dot_general x16, matrix products, pair_grads(): jnp.einsum('hqk,hqd->hkd', score_grad, query_heads, preferred_element_typ...  51.7 us
    dot_general x16, matrix products, pair_grads(): jnp.einsum('hqk,hqd->hkd', probs.astype(jnp.bfloat16), grad_heads, prefer...  51.5 us
    dot_general x16, matrix products, pair_grads(): jnp.einsum('hqk,hkd->hqd', score_grad, key_heads, preferred_element_type=...  51.3 us
    all_gather x1, waiting for transfers between devices, per_device(): lax.all_gather(out_weight, 'fsdp', axis=0, tiled=True)  48 us
    unnamed x31, local copies, waits for them, and re-layouts  23.6 us
    dynamic_slice x16, local copies, waits for them, and re-layouts, take_blocks(): value_blocks[key_block]  22.3 us
  transfers between devices with their start and end apart: 3, of which 2 were waited for; matrix products, arithmetic and copies ran while one was open for 62% of the time, Pallas kernels for 0%

commit v1 on v0

v1 whole, which is shorter than its diff:
```python
import jax
import jax.numpy as jnp
from jax import lax
from jax.experimental import pallas as pl
from jax.experimental.pallas import tpu as pltpu
from jax.sharding import PartitionSpec as P

T = 512
HW = 2048
HEADS = 16
HR = 128
SH = 8
LOG2E = 1.4426950408889634
F32 = jnp.float32
BF16 = jnp.bfloat16
MESH = pl.DeviceIdType.MESH


def dot_nn(a, b):
    return lax.dot_general(a, b, (((1,), (0,)), ((), ())), preferred_element_type=F32)


def dot_nt(a, b):
    return lax.dot_general(a, b, (((1,), (1,)), ((), ())), preferred_element_type=F32)


def dot_tn(a, b):
    return lax.dot_general(a, b, (((0,), (0,)), ((), ())), preferred_element_type=F32)


def kernel(
    q_hbm, k_hbm, v_hbm, ao_hbm, og_hbm, ln_ref, seg_ref, kept_ref, w_hbm,
    dq_hbm, dk_hbm, dv_hbm, dw_hbm,
    q_v, k_v, v_v, ao, po, g_all, aot, w_all, dwp, d_o, pg, bias, norm_t,
    ra, ta, sa, suma, ya, yra, za,
    rc, tc, sc, sumc, yc, yrc, xc,
    fin, fin_all, dw_v,
    load_sem, out_sem,
    s_core, r_core, r_pg,
    s_a, r_a1, r_ay, r_ax, r_ax2,
    s_c, r_cy, r_cz, r_cz2,
    s_rs, r_ra, r_sa, r_ya, r_za, r_rc, r_sc, r_yc, r_xc, r_fin,
):
    dp = lax.axis_index("dp")
    fs = lax.axis_index("fsdp")
    x = lax.rem(dp, 4)
    zl = lax.div(dp, 4)
    core = lax.rem(fs, 2)
    zh = lax.rem(lax.div(fs, 2), 2)
    y = lax.div(fs, 4)
    z = 2 * zh + zl
    k0 = 2 * y + zh
    zn = 3 - z

    def m4(a):
        return lax.rem(a + 8, 4)

    def dev(x_, y_, z_, c_):
        return (lax.rem(z_, 2) * 4 + x_, (y_ * 2 + lax.div(z_, 2)) * 2 + c_)

    me_partner = dev(x, y, z, 1 - core)

    def at_x(e):
        return dev(m4(x + e), y, z, core)

    def at_y(e):
        return dev(x, m4(y + e), z, core)

    def at_z(e):
        return dev(x, y, m4(z + e), core)

    def cols_a(x_):
        return pl.ds(pl.multiple_of(x_ * 256, 128), 256)

    def cols_c(zl_):
        return pl.ds(pl.multiple_of(1024 + zl_ * 512, 128), 512)

    def head_cols(h):
        return pl.ds(pl.multiple_of(h * HR, HR), HR)

    def rcopy(src, dst, ssem, rsem, to):
        return pltpu.make_async_remote_copy(src, dst, ssem, rsem, device_id=to, device_id_type=MESH)

    def arrived(dst, rsem):
        rcopy(dst, dst, rsem, rsem, me_partner).wait_recv()

    loads = {}

    def load(i, src, dst):
        c = pltpu.make_async_copy(src, dst, load_sem.at[i])
        c.start()
        loads[i] = c

    load(0, w_hbm, w_all.at[k0])
    load(1, og_hbm, g_all.at[pl.ds(0, T)])
    load(2, ao_hbm, ao)
    load(3, q_hbm, q_v)
    load(4, k_hbm, k_v)
    load(5, v_hbm, v_v)

    peers = [me_partner]
    for e in (1, 2, 3):
        peers += [at_x(e), at_y(e), at_z(e)]
    zs = 2 * zh + (1 - zl)
    final_peers = []
    for e in (0, 1, 2, 3):
        if e:
            final_peers.append(dev(m4(x + e), y, z, core))
        final_peers.append(dev(m4(x + e), y, zs, core))
        if e:
            peers.append(dev(m4(x + e), y, zs, core))
    bar = pltpu.get_barrier_semaphore()
    for p in peers:
        pl.semaphore_signal(bar, inc=1, device_id=p, device_id_type=MESH)
    pl.semaphore_wait(bar, len(peers))

    sent = []

    def send(src, dst, ssem, rsem, to):
        c = rcopy(src, dst, ssem, rsem, to)
        c.start()
        sent.append(c)

    loads[0].wait()
    ax, cz = cols_a(x), cols_c(zl)
    na = [0]

    def sem_a():
        na[0] += 1
        return s_a.at[na[0] - 1]

    nc = [0]

    def sem_c():
        nc[0] += 1
        return s_c.at[nc[0] - 1]

    def a_to_y(k, j):
        part = w_all.at[k, :, ax]
        for e in (1, 3, 2):
            send(part, part, sem_a(), r_ay.at[(4 - e) - 1, j], at_y(e))

    def a_to_x(i, k):
        part = w_all.at[k, :, ax]
        send(part, part, sem_a(), r_ax.at[0, i], at_x(1))
        send(part, part, sem_a(), r_ax.at[1, i], at_x(3))

    def a_relay(i, k):
        lcol, rcol = cols_a(m4(x - 1)), cols_a(m4(x + 1))
        arrived(w_all.at[k, :, lcol], r_ax.at[0, i])
        part = w_all.at[k, pl.ds(0, 64), lcol]
        send(part, part, sem_a(), r_ax2.at[0, i], at_x(1))
        arrived(w_all.at[k, :, rcol], r_ax.at[1, i])
        part = w_all.at[k, pl.ds(64, 64), rcol]
        send(part, part, sem_a(), r_ax2.at[1, i], at_x(3))

    def c_to_z(i, k):
        part = w_all.at[k, :, cz]
        send(part, part, sem_c(), r_cz.at[0, i], at_z(1))
        send(part, part, sem_c(), r_cz.at[1, i], at_z(3))

    def z_cols_rows(e, yy):
        zz = m4(z + e)
        return 2 * yy + lax.div(zz, 2), cols_c(lax.rem(zz, 2))

    def c_relay(i, yy):
        k, c = z_cols_rows(-1, yy)
        arrived(w_all.at[k, :, c], r_cz.at[0, i])
        part = w_all.at[k, pl.ds(0, 64), c]
        send(part, part, sem_c(), r_cz2.at[0, i], at_z(1))
        k, c = z_cols_rows(1, yy)
        arrived(w_all.at[k, :, c], r_cz.at[1, i])
        part = w_all.at[k, pl.ds(64, 64), c]
        send(part, part, sem_c(), r_cz2.at[1, i], at_z(3))

    own_a = w_all.at[k0, :, ax]
    own_c = w_all.at[k0, :, cz]
    k1 = 2 * y + 1 - zh
    send(own_a, own_a, sem_a(), r_a1.at[0], dev(x, y, zn, core))
    send(own_c, own_c, sem_c(), r_cz.at[0, 0], dev(x, y, zn, core))
    send(own_c, own_c, sem_c(), r_cz.at[1, 0], at_z(2))
    a_to_y(k0, 0)
    for e in (1, 3, 2):
        send(own_c, own_c, sem_c(), r_cy.at[(4 - e) - 1], at_y(e))

    loads[1].wait()
    segs = [seg_ref[0, b] for b in range(4)]
    kepts = [kept_ref[0, b] for b in range(4)]
    live = []
    for b in range(4):
        first = jnp.int32(0)
        kept = jnp.int32(0)
        for j in range(4):
            first = first + jnp.where(segs[j] < segs[b], 1, 0)
            kept = kept + jnp.where(segs[b] == j, kepts[j], 0)
        live.append(kept - (b - first) * 128)
    for b in range(4):
        rows = pl.ds(b * 128, 128)
        ok = lax.broadcasted_iota(jnp.int32, (128, HW), 0) < live[b]
        g_all[rows, :] = jnp.where(ok, g_all[rows, :].astype(F32), 0.0).astype(BF16)
    own_g = g_all.at[pl.ds(0, T)]
    send(own_g, g_all.at[pl.ds(T, T)], s_core.at[0], r_core.at[0], me_partner)
    loads[2].wait()
    for i in range(SH):
        send(ao.at[:, head_cols(2 * i + 1 - core)], po.at[i], s_core.at[1 + i], r_core.at[1 + i], me_partner)

    for b in range(4):
        ok = lax.broadcasted_iota(jnp.int32, (128, 128), 0) < live[b]
        for t in range(4):
            same = ok & (jnp.full((128, 128), segs[b] - segs[t]) == 0)
            bias[pl.ds(b * 128, 128), pl.ds(t * 128, 128)] = jnp.where(same, 0.0, -1e30).astype(F32)
    lanes = jnp.concatenate([ln_ref[...] * LOG2E, jnp.zeros((T, 112), F32)], axis=1)
    norm_t[...] = jnp.transpose(lanes)

    for i in range(SH):
        aot[pl.ds(i * HR, HR), pl.ds(0, T)] = jnp.transpose(ao[:, head_cols(2 * i + core)])

    arrived(w_all.at[k1, :, ax], r_a1.at[0])
    a_to_x(1, k1)
    a_to_y(k1, 1)
    arrived(w_all.at[2 * m4(y + 1) + zh, :, cz], r_cy.at[0])
    c_to_z(1, 2 * m4(y + 1) + zh)
    arrived(w_all.at[2 * m4(y + 3) + zh, :, cz], r_cy.at[2])
    c_to_z(2, 2 * m4(y + 3) + zh)

    order_a = [k0, k1]
    for e in (1, 3, 2):
        for j in (0, 1):
            order_a.append(2 * m4(y + e) + (zh if j == 0 else 1 - zh))
    y_of = [y, m4(y + 1), m4(y + 3), m4(y + 2)]

    def a_step(i):
        e = (1, 3, 2)[(i - 2) // 2]
        j = i % 2
        arrived(w_all.at[order_a[i], :, ax], r_ay.at[e - 1, j])
        a_to_x(i, order_a[i])

    a_step(2)
    a_step(4)

    for i in range(SH):
        arrived(po.at[i], r_core.at[1 + i])
        aot[pl.ds(i * HR, HR), pl.ds(T, T)] = jnp.transpose(po[i])
    arrived(g_all.at[pl.ds(T, T)], r_core.at[0])

    def dw_tiles(lo, hi):
        def body(n, carry):
            cols = pl.ds(pl.multiple_of(n * 256, 256), 256)
            part = dot_nn(aot[...], g_all[:, cols])
            dwp[:, :, cols] = part.reshape(SH, HR, 256).astype(BF16)
            return carry

        lax.fori_loop(lo, hi, body, 0)

    dw_tiles(0, 3)
    arrived(w_all.at[2 * m4(y + 2) + zh, :, cz], r_cy.at[1])
    c_to_z(3, 2 * m4(y + 2) + zh)
    a_step(6)
    a_step(3)
    a_step(5)
    a_step(7)
    a_relay(1, order_a[1])
    c_relay(1, y_of[1])
    dw_tiles(3, 6)
    c_relay(2, y_of[2])
    a_relay(2, order_a[2])
    a_relay(4, order_a[4])
    a_relay(6, order_a[6])
    dw_tiles(6, 8)
    for i in (3, 5, 7):
        a_relay(i, order_a[i])
    c_relay(3, y_of[3])

    nr = [0]

    def sem_rs():
        nr[0] += 1
        return s_rs.at[nr[0] - 1]

    dwz = dwp
    half = (pl.ds(0, 4), pl.ds(4, 4))
    xr, xl, x2 = m4(x + 1), m4(x + 3), m4(x + 2)
    send(dwz.at[half[0], :, cols_a(x2)], ra.at[0], sem_rs(), r_ra.at[0], at_x(1))
    send(dwz.at[half[1], :, cols_a(x2)], ra.at[1], sem_rs(), r_ra.at[1], at_x(3))

    def c_rows(e, hf):
        zz = m4(z + e)
        return lax.div(zz, 2), cols_c(lax.rem(zz, 2))

    def send_c(e, ys, dst, base, rsem, r0, to):
        zhh, c = c_rows(e, None)
        for n, yy in enumerate(ys):
            send(dwz.at[2 * yy + zhh, :, c], dst.at[base + n], sem_rs(), rsem.at[r0 + n], to)

    send_c(2, (0, 1), rc.at[0], 0, r_rc, 0, at_z(1))
    send_c(2, (2, 3), rc.at[1], 0, r_rc, 2, at_z(3))
    send(dwz.at[half[1], :, cols_a(xr)], sa.at[0, half[1]], sem_rs(), r_sa.at[0, 1], at_x(1))
    send(dwz.at[half[0], :, cols_a(xl)], sa.at[1, half[0]], sem_rs(), r_sa.at[1, 0], at_x(3))
    send_c(1, (2, 3), sc.at[0], 2, r_sc, 2, at_z(1))
    send_c(3, (0, 1), sc.at[1], 0, r_sc, 4, at_z(3))

    for i in range(1, 8):
        k = order_a[i]
        arrived(w_all.at[k, pl.ds(0, 64), cols_a(m4(x + 2))], r_ax2.at[0, i])
        arrived(w_all.at[k, pl.ds(64, 64), cols_a(m4(x + 2))], r_ax2.at[1, i])
    arrived(w_all.at[k1, :, cols_c(1 - zl)], r_cz.at[0, 0])
    arrived(w_all.at[k1, :, cz], r_cz.at[1, 0])
    for i in range(1, 4):
        k, c = z_cols_rows(2, y_of[i])
        arrived(w_all.at[k, pl.ds(0, 64), c], r_cz2.at[0, i])
        arrived(w_all.at[k, pl.ds(64, 64), c], r_cz2.at[1, i])

    for i in range(4):
        wt = w_all[pl.ds(2 * i, 2)].reshape(2 * HR, HW)
        for part in (1, 0):
            got = dot_nt(g_all[pl.ds(part * T, T), :], wt).astype(BF16)
            for j in range(2):
                piece = got[:, j * HR : (j + 1) * HR]
                if part == 0:
                    d_o[2 * (2 * i + j) + core] = piece
                else:
                    pg[2 * i + j] = piece
                    send(pg.at[2 * i + j], d_o.at[2 * (2 * i + j) + core], s_core.at[9 + 2 * i + j], r_pg.at[2 * i + j], me_partner)

    scale = HR ** -0.5
    loads[3].wait()
    loads[4].wait()
    loads[5].wait()

    def attention(parity, lo, hi):
        def body(i, carry):
            h = 2 * i + parity
            hc = head_cols(h)
            qh, kh, vh = q_v[:, hc], k_v[:, hc], v_v[:, hc]
            gh = d_o[h]
            both = gh.astype(F32) * ao[:, hc].astype(F32)
            delta = jnp.sum(jnp.transpose(both), axis=0, keepdims=True)
            norm = norm_t[pl.ds(h, 1), :]
            s = dot_nt(kh, qh) * (scale * LOG2E) - norm + bias[...]
            p = jnp.exp2(s)
            dv = dot_nn(p.astype(BF16), gh)
            ds = (p * (dot_nt(vh, gh) - delta)).astype(BF16)
            dk = dot_nn(ds, qh) * scale
            dq = dot_tn(ds, kh) * scale
            q_v[:, hc] = dq.astype(BF16)
            k_v[:, hc] = dk.astype(BF16)
            v_v[:, hc] = dv.astype(BF16)
            return carry

        lax.fori_loop(lo, hi, body, 0)

    attention(core, 0, 2)

    def relay_a(d):
        arrived(ra.at[d], r_ra.at[d])
        to = xr if d == 0 else xl
        ta[d] = (dwp[half[d], :, cols_a(to)].astype(F32) + ra[d].astype(F32)).astype(BF16)
        send(ta.at[d], sa.at[d, half[d]], sem_rs(), r_sa.at[d, d], at_x(1 if d == 0 else 3))

    def relay_c(d):
        zhh, c = c_rows(1 if d == 0 else 3, None)
        for n in range(2):
            yy = 2 * d + n
            arrived(rc.at[d, n], r_rc.at[2 * d + n])
            tc[d, n] = (dwp[2 * yy + zhh, :, c].astype(F32) + rc[d, n].astype(F32)).astype(BF16)
            send(tc.at[d, n], sc.at[d, yy], sem_rs(), r_sc.at[4 * d + yy], at_z(1 if d == 0 else 3))

    for d in (0, 1):
        relay_a(d)
        relay_c(d)

    attention(core, 2, 7)

    for d in (0, 1):
        arrived(sa.at[d, half[0]], r_sa.at[d, 0])
        arrived(sa.at[d, half[1]], r_sa.at[d, 1])
    for yy in range(4):
        rows = pl.ds(2 * yy, 2)
        suma[rows] = (
            dwp[rows, :, ax].astype(F32) + sa[0, rows].astype(F32) + sa[1, rows].astype(F32)
        ).astype(BF16)
    for e in (1, 3, 2):
        rows = pl.ds(2 * m4(y + e), 2)
        send(suma.at[rows], ya.at[(4 - e) - 1], sem_rs(), r_ya.at[(4 - e) - 1], at_y(e))
    for d in (0, 1):
        for yy in range(4):
            arrived(sc.at[d, yy], r_sc.at[4 * d + yy])
    for yy in range(4):
        sumc[yy] = (
            dwp[2 * yy + zh, :, cz].astype(F32) + sc[0, yy].astype(F32) + sc[1, yy].astype(F32)
        ).astype(BF16)
    for e in (1, 3, 2):
        send(sumc.at[m4(y + e)], yc.at[(4 - e) - 1], sem_rs(), r_yc.at[(4 - e) - 1], at_y(e))

    attention(core, 7, 8)
    for i in range(SH):
        arrived(d_o.at[2 * i + 1 - core], r_pg.at[i])
    attention(1 - core, 0, 2)

    for e in (1, 2, 3):
        arrived(ya.at[e - 1], r_ya.at[e - 1])
        arrived(yc.at[e - 1], r_yc.at[e - 1])
    tot = suma[pl.ds(2 * y, 2)].astype(F32)
    totc = sumc[y].astype(F32)
    for e in range(3):
        tot = tot + ya[e].astype(F32)
        totc = totc + yc[e].astype(F32)
    yra[...] = tot.astype(BF16)
    yrc[...] = totc.astype(BF16)

    def quarter(i):
        return pl.ds(pl.multiple_of(i * HR, HR), HR)

    for e in (1, 3, 2):
        zz = m4(z + e)
        send(yra.at[lax.div(zz, 2), :, quarter(lax.rem(zz, 2))], za.at[(4 - e) - 1], sem_rs(), r_za.at[(4 - e) - 1], at_z(e))
        send(yrc.at[:, quarter(m4(x + e))], xc.at[(4 - e) - 1], sem_rs(), r_xc.at[(4 - e) - 1], at_x(e))

    attention(1 - core, 2, 4)

    for e in range(3):
        arrived(za.at[e], r_za.at[e])
        arrived(xc.at[e], r_xc.at[e])
    tot = yra[zh, :, quarter(zl)].astype(F32)
    totc = yrc[:, quarter(x)].astype(F32)
    for e in range(3):
        tot = tot + za[e].astype(F32)
        totc = totc + xc[e].astype(F32)
    fin[0] = tot.astype(BF16)
    fin[1] = totc.astype(BF16)
    slot = 0
    for e in range(4):
        for f in (0, 1):
            if e == 0 and f == 0:
                continue
            to = dev(m4(x + e), y, z if f == 0 else zs, core)
            at = ((4 - e) % 4) * 2 + f
            send(fin, fin_all.at[at], sem_rs(), r_fin.at[at], to)
            slot += 1

    attention(1 - core, 4, 8)

    for i, (src, dst) in enumerate(((q_v, dq_hbm), (k_v, dk_hbm), (v_v, dv_hbm))):
        pltpu.make_async_copy(src, dst, out_sem.at[i]).start()

    for e in range(4):
        for f in (0, 1):
            at = e * 2 + f
            if at:
                arrived(fin_all.at[at], r_fin.at[at])
                block = fin_all[at]
            else:
                block = fin[...]
            xx = m4(x + e)
            zz = zl if f == 0 else 1 - zl
            dw_v[:, pl.ds(pl.multiple_of(256 * xx + 128 * zz, 128), 128)] = block[0].astype(F32)
            dw_v[:, pl.ds(pl.multiple_of(1024 + 512 * zz + 128 * xx, 128), 128)] = block[1].astype(F32)
    pltpu.make_async_copy(dw_v, dw_hbm, out_sem.at[3]).start()

    for c in sent:
        c.wait_send()
    for i, (src, dst) in enumerate(((q_v, dq_hbm), (k_v, dk_hbm), (v_v, dv_hbm), (dw_v, dw_hbm))):
        pltpu.make_async_copy(src, dst, out_sem.at[i]).wait()


def per_device(queries, keys, values, attn_out, out_grad, log_norm, segment_ids, kept_tokens, out_weight):
    hbm = pl.BlockSpec(memory_space=pl.ANY)
    vmem = pl.BlockSpec(memory_space=pltpu.VMEM)
    smem = pl.BlockSpec(memory_space=pltpu.SMEM)
    dma = pltpu.SemaphoreType.DMA
    tok = jax.ShapeDtypeStruct((T, HW), BF16)
    V = pltpu.VMEM
    scratch = [
        V((T, HW), BF16), V((T, HW), BF16), V((T, HW), BF16),
        V((T, HW), BF16), V((SH, T, HR), BF16),
        V((2 * T, HW), BF16), V((SH * HR, 2 * T), BF16),
        V((SH, HR, HW), BF16), V((SH, HR, HW), BF16),
        V((HEADS, T, HR), BF16), V((SH, T, HR), BF16),
        V((T, T), F32), V((HR, T), F32),
        V((2, 4, HR, 256), BF16), V((2, 4, HR, 256), BF16), V((2, SH, HR, 256), BF16),
        V((SH, HR, 256), BF16), V((3, 2, HR, 256), BF16), V((2, HR, 256), BF16), V((3, HR, HR), BF16),
        V((2, 2, HR, 512), BF16), V((2, 2, HR, 512), BF16), V((2, 4, HR, 512), BF16),
        V((4, HR, 512), BF16), V((3, HR, 512), BF16), V((HR, 512), BF16), V((3, HR, HR), BF16),
        V((2, HR, HR), BF16), V((8, 2, HR, HR), BF16), V((HR, HW), F32),
        dma((6,)), dma((4,)),
        dma((17,)), dma((9,)), dma((8,)),
        dma((48,)), dma((1,)), dma((3, 2)), dma((2, 8)), dma((2, 8)),
        dma((20,)), dma((3,)), dma((2, 4)), dma((2, 4)),
        dma((48,)), dma((2,)), dma((2, 2)), dma((3,)), dma((3,)),
        dma((4,)), dma((8,)), dma((3,)), dma((3,)), dma((8,)),
    ]
    return pl.pallas_call(
        kernel,
        out_shape=(tok, tok, tok, jax.ShapeDtypeStruct((HR, HW), F32)),
        in_specs=[hbm] * 5 + [vmem, smem, smem, hbm],
        out_specs=(hbm,) * 4,
        scratch_shapes=scratch,
        compiler_params=pltpu.CompilerParams(
            collective_id=0, has_side_effects=True, vmem_limit_bytes=62 * 2**20
        ),
    )(queries, keys, values, attn_out, out_grad, log_norm, segment_ids, kept_tokens, out_weight)


def solution(mesh):
    token = P(("dp", "fsdp"), None)
    return jax.shard_map(
        per_device,
        mesh=mesh,
        in_specs=(token,) * 8 + (P("fsdp", None),),
        out_specs=(token, token, token, P("fsdp", None)),
        check_vma=False,
    )
```

time: 487 us -> 86.1 us (0.18)
  matrix products: 192 us -> 0 us
  waiting for transfers between devices: 107 us -> 0 us
  local copies, waits for them, and re-layouts: 92.4 us -> 10.2 us
  Pallas kernels: 0 us -> 75 us
  loops' own time: 53.1 us -> 0 us
  other arithmetic: 23.7 us -> 0 us
  between operations: 14 us -> 0.65 us
    dot_general x82 -> x0, matrix products: 192 us -> none  [the longest x16 51.7 us: pair_grads(): jnp.einsum('hqk,hqd->hkd', score_grad, query_heads, preferred_element_typ...]
    pallas_call x0 -> x1, Pallas kernels: none -> 75 us  [per_device(): pl.pallas_call(kernel, out_shape=(tok, tok, tok, jax.ShapeDtypeStruct((HR...]
    psum x1 -> x0, waiting for transfers between devices: 58 us -> none  [per_device(): weight_grad = lax.psum(grad_share, 'dp')]
    another operation x1 -> x0, loops' own time: 53.1 us -> none  [per_device(): totals = lax.fori_loop(0, pair_total, run_pair, totals)]
    dynamic_slice x64 -> x0, local copies, waits for them, and re-layouts: 49.9 us -> none  [the longest x16 22.3 us: take_blocks(): value_blocks[key_block]]
    all_gather x1 -> x0, waiting for transfers between devices: 48 us -> none  [per_device(): lax.all_gather(out_weight, 'fsdp', axis=0, tiled=True)]
    unnamed x31 -> x11, local copies, waits for them, and re-layouts: 23.6 us -> 10.2 us
    another operation x16 -> x0, other arithmetic: 12.5 us -> none
  transfers between devices with their start and end apart: 3 -> 0, of which waited for: 2 -> 0; matrix products, arithmetic and copies ran while one was open for 62% -> 0% of each run, Pallas kernels for 0% -> 0%
where the time goes in v1:
time: 86.1 us; the launch traced here: 85.8 us
  Pallas kernels  75 us (87%)
  local copies, waits for them, and re-layouts  10.2 us (12%)
    pallas_call x1, Pallas kernels, per_device(): pl.pallas_call(kernel, out_shape=(tok, tok, tok, jax.ShapeDtypeStruct((HR...  75 us
    unnamed x11, local copies, waits for them, and re-layouts  10.2 us

profile of v1, /device:TPU:0, one launch (start us, length us, event | category | flops | bytes accessed | tf_op | source)
XLA Modules:
  0.0 85.8 jit_solution(9448785483798251840)
XLA Ops:
  0.6 1.6 %copy.13.ln_ref = f32[512,16]{1,0:T(8,128)} copy(f32[512,16]{0,1:T(8,128)} %param.14) | data formatting | bytes 65536 | tf_op args[5]
  2.2 75.0 %shard_map.120 = (bf16[512,2048]{1,0:T(8,128)(2,1)}, bf16[512,2048]{1,0:T(8,128)(2,1)}, bf16[512,2048]{1,0:T(8,128)(2,1)}, f32[128,2048]{1,0:T(8,128)}) custom-call(bf16[512,2048]{1,0:T(8,128)(2,1)} %q_hbm.1, bf16[512,2048]{1,0:T(8,128)(2,1)} %k_hbm.1, bf16[512,2048]{1,0:T(8,128)(2,1)} %v_hbm.1, bf16[512,2048]{1,0:T(8,128)(2,1)} %ao_hbm.1, ...), custom_call_target="tpu_custom_call" | custom-call | tf_op jit(solution)/shard_map/pallas_call | solution.py:492
  77.2 0.0 copy-start.1
  77.3 3.3 %copy.18 = bf16[512,2048]{1,0:T(8,128)(2,1)} copy(bf16[512,2048]{1,0:T(8,128)(2,1)} %get-tuple-element.8) | data formatting | bytes 4194304
  80.6 0.0 copy-done.1
  80.6 0.0 copy-start
  80.6 1.3 %copy.19 = bf16[512,2048]{1,0:T(8,128)(2,1)} copy(bf16[512,2048]{1,0:T(8,128)(2,1)S(1)} %copy-done.1) | data formatting | bytes 4194304
  81.9 1.0 %copy-done = bf16[512,2048]{1,0:T(8,128)(2,1)S(1)} copy-done((bf16[512,2048]{1,0:T(8,128)(2,1)S(1)}, bf16[512,2048]{1,0:T(8,128)(2,1)}, u32[]{:S(2)}) %copy-start) | copy-done | bytes 2097176
  82.9 0.0 copy-start.2
  82.9 1.3 %copy.20 = bf16[512,2048]{1,0:T(8,128)(2,1)} copy(bf16[512,2048]{1,0:T(8,128)(2,1)S(1)} %copy-done) | data formatting | bytes 4194304
  84.2 0.6 copy-done.2
  84.9 1.0 %copy.21 = f32[128,2048]{1,0:T(8,128)} copy(f32[128,2048]{1,0:T(8,128)S(1)} %copy-done.2) | data formatting | bytes 2097152
Async XLA Ops:
  77.2 3.3 %copy-start.1 = (bf16[512,2048]{1,0:T(8,128)(2,1)S(1)}, bf16[512,2048]{1,0:T(8,128)(2,1)}, u32[]{:S(2)}) copy-start(bf16[512,2048]{1,0:T(8,128)(2,1)} %get-tuple-element.9) | copy-start | bytes 6291460
  80.6 2.3 %copy-start = (bf16[512,2048]{1,0:T(8,128)(2,1)S(1)}, bf16[512,2048]{1,0:T(8,128)(2,1)}, u32[]{:S(2)}) copy-start(bf16[512,2048]{1,0:T(8,128)(2,1)} %get-tuple-element.10) | copy-start | bytes 6291460
  82.9 2.0 %copy-start.2 = (f32[128,2048]{1,0:T(8,128)S(1)}, f32[128,2048]{1,0:T(8,128)}, u32[]{:S(2)}) copy-start(f32[128,2048]{1,0:T(8,128)} %get-tuple-element.11) | copy-start | bytes 3145732

commit v2 on v1

v2 whole, which is shorter than its diff:
```python
import jax
import jax.numpy as jnp
from jax import lax
from jax.experimental import pallas as pl
from jax.experimental.pallas import tpu as pltpu
from jax.sharding import PartitionSpec as P

T = 512
HW = 2048
HEADS = 16
HR = 128
SH = 8
LOG2E = 1.4426950408889634
F32 = jnp.float32
BF16 = jnp.bfloat16
MESH = pl.DeviceIdType.MESH


def dot_nn(a, b):
    return lax.dot_general(a, b, (((1,), (0,)), ((), ())), preferred_element_type=F32)


def dot_nt(a, b):
    return lax.dot_general(a, b, (((1,), (1,)), ((), ())), preferred_element_type=F32)


def dot_tn(a, b):
    return lax.dot_general(a, b, (((0,), (0,)), ((), ())), preferred_element_type=F32)


def kernel(
    q_hbm, k_hbm, v_hbm, ao_hbm, og_hbm, ln_hbm, seg_hbm, kept_hbm, w_hbm,
    dq_hbm, dk_hbm, dv_hbm, dw_hbm,
    q_v, k_v, v_v, ao, po, g_all, aot, w_all, dwp, d_o, pg, bias, norm_t, seg_ref, kept_ref,
    ra, ta, sa, suma, ya, yra, za,
    rc, tc, sc, sumc, yc, yrc, xc,
    fin, fin_all, dw_v,
    load_sem, out_sem, dw_sem,
    s_core, r_core, r_pg,
    s_a, r_a1, r_ay, r_ax, r_ax2,
    s_c, r_cy, r_cz, r_cz2,
    s_rs, r_ra, r_sa, r_ya, r_za, r_rc, r_sc, r_yc, r_xc, r_fin,
):
    dp = lax.axis_index("dp")
    fs = lax.axis_index("fsdp")
    x = lax.rem(dp, 4)
    zl = lax.div(dp, 4)
    core = lax.rem(fs, 2)
    zh = lax.rem(lax.div(fs, 2), 2)
    y = lax.div(fs, 4)
    z = 2 * zh + zl
    k0 = 2 * y + zh
    zn = 3 - z

    def m4(a):
        return lax.rem(a + 8, 4)

    def dev(x_, y_, z_, c_):
        return (lax.rem(z_, 2) * 4 + x_, (y_ * 2 + lax.div(z_, 2)) * 2 + c_)

    me_partner = dev(x, y, z, 1 - core)

    def at_x(e):
        return dev(m4(x + e), y, z, core)

    def at_y(e):
        return dev(x, m4(y + e), z, core)

    def at_z(e):
        return dev(x, y, m4(z + e), core)

    def cols_a(x_):
        return pl.ds(pl.multiple_of(x_ * 256, 128), 256)

    def cols_c(zl_):
        return pl.ds(pl.multiple_of(1024 + zl_ * 512, 128), 512)

    def head_cols(h):
        return pl.ds(pl.multiple_of(h * HR, HR), HR)

    def rcopy(src, dst, ssem, rsem, to):
        return pltpu.make_async_remote_copy(src, dst, ssem, rsem, device_id=to, device_id_type=MESH)

    def arrived(dst, rsem):
        rcopy(dst, dst, rsem, rsem, me_partner).wait_recv()

    loads = []

    def load(src, dst):
        c = pltpu.make_async_copy(src, dst, load_sem.at[len(loads)])
        c.start()
        loads.append(c)
        return c

    l_w = load(w_hbm, w_all.at[k0])
    l_seg = load(seg_hbm, seg_ref)
    l_kept = load(kept_hbm, kept_ref)
    l_g = load(og_hbm, g_all.at[pl.ds(0, T)])
    l_ao = load(ao_hbm, ao)
    l_ln = load(ln_hbm, norm_t)
    l_q = load(q_hbm, q_v)
    l_k = load(k_hbm, k_v)
    l_v = load(v_hbm, v_v)

    zs = 2 * zh + (1 - zl)
    peers = [me_partner]
    for e in (1, 2, 3):
        peers += [at_x(e), at_y(e), at_z(e), dev(m4(x + e), y, zs, core)]
    bar = pltpu.get_barrier_semaphore()
    for p in peers:
        pl.semaphore_signal(bar, inc=1, device_id=p, device_id_type=MESH)
    pl.semaphore_wait(bar, len(peers))

    sent = []
    used = {"a": 0, "c": 0, "rs": 0}
    send_sems = {"a": s_a, "c": s_c, "rs": s_rs}

    def send(src, dst, ssem, rsem, to):
        if isinstance(ssem, str):
            used[ssem] += 1
            ssem = send_sems[ssem].at[used[ssem] - 1]
        c = rcopy(src, dst, ssem, rsem, to)
        c.start()
        sent.append(c)

    l_w.wait()
    ax, cz = cols_a(x), cols_c(zl)
    k1 = 2 * y + 1 - zh
    ORDER = (1, 3, 2)

    def row_k(e, j):
        return 2 * m4(y + e) + (zh if j == 0 else 1 - zh)

    def a_to_y(k, j, es):
        part = w_all.at[k, :, ax]
        for e in es:
            send(part, part, "a", r_ay.at[(4 - e) - 1, j], at_y(e))

    def c_to_y(es):
        part = w_all.at[k0, :, cz]
        for e in es:
            send(part, part, "c", r_cy.at[(4 - e) - 1], at_y(e))

    def a_to_x(e, j):
        k = row_k(e, j)
        part = w_all.at[k, :, ax]
        send(part, part, "a", r_ax.at[0, e, j], at_x(1))
        send(part, part, "a", r_ax.at[1, e, j], at_x(3))

    def a_relay(e, j):
        k = row_k(e, j)
        lcol, rcol = cols_a(m4(x - 1)), cols_a(m4(x + 1))
        arrived(w_all.at[k, :, lcol], r_ax.at[0, e, j])
        part = w_all.at[k, pl.ds(0, 64), lcol]
        send(part, part, "a", r_ax2.at[0, e, j], at_x(1))
        arrived(w_all.at[k, :, rcol], r_ax.at[1, e, j])
        part = w_all.at[k, pl.ds(64, 64), rcol]
        send(part, part, "a", r_ax2.at[1, e, j], at_x(3))

    def z_place(ez, e):
        zz = m4(z + ez)
        return 2 * m4(y + e) + lax.div(zz, 2), cols_c(lax.rem(zz, 2))

    def c_to_z(e):
        part = w_all.at[row_k(e, 0), :, cz]
        send(part, part, "c", r_cz.at[0, e], at_z(1))
        send(part, part, "c", r_cz.at[1, e], at_z(3))

    def c_relay(e):
        k, c = z_place(-1, e)
        arrived(w_all.at[k, :, c], r_cz.at[0, e])
        part = w_all.at[k, pl.ds(0, 64), c]
        send(part, part, "c", r_cz2.at[0, e], at_z(1))
        k, c = z_place(1, e)
        arrived(w_all.at[k, :, c], r_cz.at[1, e])
        part = w_all.at[k, pl.ds(64, 64), c]
        send(part, part, "c", r_cz2.at[1, e], at_z(3))

    def a_step(e, j):
        arrived(w_all.at[row_k(e, j), :, ax], r_ay.at[e - 1, j])
        a_to_x(e, j)

    def c_step(e):
        arrived(w_all.at[row_k(e, 0), :, cz], r_cy.at[e - 1])
        c_to_z(e)

    own_a = w_all.at[k0, :, ax]
    own_c = w_all.at[k0, :, cz]
    send(own_a, own_a, "a", r_a1.at[0], dev(x, y, zn, core))
    a_to_y(k0, 0, (1, 3))
    c_to_y((1, 3))
    a_to_y(k0, 0, (2,))
    c_to_y((2,))
    send(own_c, own_c, "c", r_cz.at[0, 0], dev(x, y, zn, core))
    send(own_c, own_c, "c", r_cz.at[1, 0], at_z(2))

    l_seg.wait()
    l_kept.wait()
    segs = [seg_ref[0, b] for b in range(4)]
    kepts = [kept_ref[0, b] for b in range(4)]
    live = []
    for b in range(4):
        first = jnp.int32(0)
        kept = jnp.int32(0)
        for j in range(4):
            first = first + jnp.where(segs[j] < segs[b], 1, 0)
            kept = kept + jnp.where(segs[b] == j, kepts[j], 0)
        live.append(kept - (b - first) * 128)
    l_g.wait()
    for b in range(4):
        rows = pl.ds(b * 128, 128)
        ok = lax.broadcasted_iota(jnp.int32, (128, HW), 0) < live[b]
        g_all[rows, :] = jnp.where(ok, g_all[rows, :].astype(F32), 0.0).astype(BF16)
    own_g = g_all.at[pl.ds(0, T)]
    send(own_g, g_all.at[pl.ds(T, T)], s_core.at[0], r_core.at[0], me_partner)
    l_ao.wait()
    for i in range(SH):
        send(ao.at[:, head_cols(2 * i + 1 - core)], po.at[i], s_core.at[1 + i], r_core.at[1 + i], me_partner)

    arrived(w_all.at[k1, :, ax], r_a1.at[0])
    a_to_y(k1, 1, ORDER)
    a_to_x(0, 1)

    def flip_own(lo, hi):
        for i in range(lo, hi):
            aot[pl.ds(i * HR, HR), pl.ds(0, T)] = jnp.transpose(ao[:, head_cols(2 * i + core)])

    flip_own(0, 2)
    a_step(1, 0)
    a_step(3, 0)
    flip_own(2, 4)
    c_step(1)
    c_step(3)
    flip_own(4, 6)
    a_step(2, 0)
    c_step(2)
    a_relay(0, 1)
    flip_own(6, 8)
    a_relay(1, 0)
    a_relay(3, 0)

    def flip_other(lo, hi):
        for i in range(lo, hi):
            arrived(po.at[i], r_core.at[1 + i])
            aot[pl.ds(i * HR, HR), pl.ds(T, T)] = jnp.transpose(po[i])

    arrived(g_all.at[pl.ds(T, T)], r_core.at[0])
    flip_other(0, 4)
    c_relay(1)
    c_relay(3)
    a_step(1, 1)
    a_step(3, 1)
    flip_other(4, 8)
    a_step(2, 1)

    def dw_group(e):
        rows = pl.ds(pl.multiple_of(2 * m4(y + e) * HR, 2 * HR), 2 * HR)

        def body(n, carry):
            cols = pl.ds(pl.multiple_of(n * 512, 512), 512)
            part = dot_nn(aot[rows, :], g_all[:, cols])
            dwp[pl.ds(2 * m4(y + e), 2), :, cols] = part.reshape(2, HR, 512).astype(BF16)
            return carry

        lax.fori_loop(0, 4, body, 0)

    xr, xl, x2 = m4(x + 1), m4(x + 3), m4(x + 2)
    top, low = pl.ds(0, 64), pl.ds(64, 64)

    def hop_far(e):
        for d in (0, 1):
            to_x, to_z = (at_x(1), at_z(1)) if d == 0 else (at_x(3), at_z(3))
            send(dwp.at[2 * m4(y + e) + d, :, cols_a(x2)], ra.at[d, e], "rs", r_ra.at[d, e], to_x)
            k, c = z_place(2, e)
            send(dwp.at[k, top if d == 0 else low, c], rc.at[d, e], "rs", r_rc.at[d, e], to_z)

    def hop_near(e):
        for d in (0, 1):
            to_x, to_z = (at_x(1), at_z(1)) if d == 0 else (at_x(3), at_z(3))
            f = 1 - d
            send(dwp.at[2 * m4(y + e) + f, :, cols_a(xr if d == 0 else xl)], sa.at[d, e, f], "rs", r_sa.at[d, e, f], to_x)
            k, c = z_place(1 if d == 0 else 3, e)
            part = low if d == 0 else top
            send(dwp.at[k, part, c], sc.at[d, e, part], "rs", r_sc.at[d, e, f], to_z)

    def hop_relay(e):
        for d in (0, 1):
            to_x, to_z = (at_x(1), at_z(1)) if d == 0 else (at_x(3), at_z(3))
            arrived(ra.at[d, e], r_ra.at[d, e])
            near = dwp[2 * m4(y + e) + d, :, cols_a(xr if d == 0 else xl)]
            ta[d, e] = (near.astype(F32) + ra[d, e].astype(F32)).astype(BF16)
            send(ta.at[d, e], sa.at[d, e, d], "rs", r_sa.at[d, e, d], to_x)
            arrived(rc.at[d, e], r_rc.at[d, e])
            k, c = z_place(1 if d == 0 else 3, e)
            part = top if d == 0 else low
            tc[d, e] = (dwp[k, part, c].astype(F32) + rc[d, e].astype(F32)).astype(BF16)
            send(tc.at[d, e], sc.at[d, e, part], "rs", r_sc.at[d, e, d], to_z)

    def hop_sum(e):
        for d in (0, 1):
            for f in (0, 1):
                arrived(sa.at[d, e, f], r_sa.at[d, e, f])
        own = dwp[pl.ds(2 * m4(y + e), 2), :, ax]
        suma[e] = (own.astype(F32) + sa[0, e].astype(F32) + sa[1, e].astype(F32)).astype(BF16)
        if e:
            send(suma.at[e], ya.at[(4 - e) - 1], "rs", r_ya.at[(4 - e) - 1], at_y(e))
        for d in (0, 1):
            for f in (0, 1):
                part = top if f == 0 else low
                arrived(sc.at[d, e, part], r_sc.at[d, e, f])
        own = dwp[2 * m4(y + e) + zh, :, cz]
        sumc[e] = (own.astype(F32) + sc[0, e].astype(F32) + sc[1, e].astype(F32)).astype(BF16)
        if e:
            send(sumc.at[e], yc.at[(4 - e) - 1], "rs", r_yc.at[(4 - e) - 1], at_y(e))

    dw_group(2)
    hop_far(2)
    hop_near(2)
    a_relay(2, 0)
    c_relay(2)
    dw_group(1)
    hop_far(1)
    hop_near(1)
    for e in ORDER:
        a_relay(e, 1)
    dw_group(3)
    hop_far(3)
    hop_near(3)
    hop_relay(2)
    dw_group(0)
    hop_far(0)
    hop_near(0)

    for b in range(4):
        ok = lax.broadcasted_iota(jnp.int32, (128, 128), 0) < live[b]
        for t in range(4):
            same = ok & (jnp.full((128, 128), segs[b] - segs[t]) == 0)
            bias[pl.ds(b * 128, 128), pl.ds(t * 128, 128)] = jnp.where(same, 0.0, -1e30).astype(F32)
    l_ln.wait()
    norm_t[...] = norm_t[...] * LOG2E

    far_a = cols_a(x2)
    for e in (0,) + ORDER:
        for j in (0, 1):
            if e or j:
                arrived(w_all.at[row_k(e, j), pl.ds(0, 64), far_a], r_ax2.at[0, e, j])
                arrived(w_all.at[row_k(e, j), pl.ds(64, 64), far_a], r_ax2.at[1, e, j])
    arrived(w_all.at[k1, :, cols_c(1 - zl)], r_cz.at[0, 0])
    arrived(w_all.at[k1, :, cz], r_cz.at[1, 0])
    for e in ORDER:
        k, c = z_place(2, e)
        arrived(w_all.at[k, pl.ds(0, 64), c], r_cz2.at[0, e])
        arrived(w_all.at[k, pl.ds(64, 64), c], r_cz2.at[1, e])

    for i in range(4):
        wt = w_all[pl.ds(2 * i, 2)].reshape(2 * HR, HW)
        for part in (1, 0):
            got = dot_nt(g_all[pl.ds(part * T, T), :], wt).astype(BF16)
            for j in range(2):
                piece = got[:, j * HR : (j + 1) * HR]
                if part == 0:
                    d_o[2 * (2 * i + j) + core] = piece
                else:
                    pg[2 * i + j] = piece
                    send(pg.at[2 * i + j], d_o.at[2 * (2 * i + j) + core], s_core.at[9 + 2 * i + j], r_pg.at[2 * i + j], me_partner)

    scale = HR ** -0.5
    l_q.wait()
    l_k.wait()
    l_v.wait()
    hop_relay(1)

    def attention(parity, lo, hi):
        def body(i, carry):
            h = 2 * i + parity
            hc = head_cols(h)
            qh, kh, vh = q_v[:, hc], k_v[:, hc], v_v[:, hc]
            gh = d_o[h]
            both = gh.astype(F32) * ao[:, hc].astype(F32)
            delta = jnp.sum(jnp.transpose(both), axis=0, keepdims=True)
            norm = norm_t[pl.ds(h, 1), :]
            s = dot_nt(kh, qh) * (scale * LOG2E) - norm + bias[...]
            p = jnp.exp2(s)
            dv = dot_nn(p.astype(BF16), gh)
            ds = (p * (dot_nt(vh, gh) - delta)).astype(BF16)
            dk = dot_nn(ds, qh) * scale
            dq = dot_tn(ds, kh) * scale
            q_v[:, hc] = dq.astype(BF16)
            k_v[:, hc] = dk.astype(BF16)
            v_v[:, hc] = dv.astype(BF16)
            pltpu.make_async_copy(q_v.at[:, hc], dq_hbm.at[:, hc], out_sem.at[0, h]).start()
            pltpu.make_async_copy(k_v.at[:, hc], dk_hbm.at[:, hc], out_sem.at[1, h]).start()
            pltpu.make_async_copy(v_v.at[:, hc], dv_hbm.at[:, hc], out_sem.at[2, h]).start()
            return carry

        lax.fori_loop(lo, hi, body, 0)

    attention(core, 0, 1)
    hop_relay(3)
    hop_sum(2)
    attention(core, 1, 2)
    hop_relay(0)
    attention(core, 2, 4)
    hop_sum(1)
    attention(core, 4, 6)
    hop_sum(3)
    attention(core, 6, 8)
    hop_sum(0)

    for i in range(SH):
        arrived(d_o.at[2 * i + 1 - core], r_pg.at[i])
    attention(1 - core, 0, 1)

    tot = suma[0].astype(F32)
    totc = sumc[0].astype(F32)
    for e in (2, 1, 3):
        arrived(ya.at[e - 1], r_ya.at[e - 1])
        tot = tot + ya[e - 1].astype(F32)
        arrived(yc.at[e - 1], r_yc.at[e - 1])
        totc = totc + yc[e - 1].astype(F32)
    yra[...] = tot.astype(BF16)
    yrc[...] = totc.astype(BF16)

    def quarter(i):
        return pl.ds(pl.multiple_of(i * HR, HR), HR)

    for e in (1, 3, 2):
        zz = m4(z + e)
        send(yra.at[lax.div(zz, 2), :, quarter(lax.rem(zz, 2))], za.at[(4 - e) - 1], "rs", r_za.at[(4 - e) - 1], at_z(e))
        send(yrc.at[:, quarter(m4(x + e))], xc.at[(4 - e) - 1], "rs", r_xc.at[(4 - e) - 1], at_x(e))

    attention(1 - core, 1, 3)

    for e in range(3):
        arrived(za.at[e], r_za.at[e])
        arrived(xc.at[e], r_xc.at[e])
    tot = yra[zh, :, quarter(zl)].astype(F32)
    totc = yrc[:, quarter(x)].astype(F32)
    for e in range(3):
        tot = tot + za[e].astype(F32)
        totc = totc + xc[e].astype(F32)
    fin[0] = tot.astype(BF16)
    fin[1] = totc.astype(BF16)
    for e in range(4):
        for f in (0, 1):
            if e or f:
                at = ((4 - e) % 4) * 2 + f
                send(fin, fin_all.at[at], "rs", r_fin.at[at], dev(m4(x + e), y, z if f == 0 else zs, core))

    attention(1 - core, 3, 8)

    for e in range(4):
        for f in (0, 1):
            at = e * 2 + f
            if at:
                arrived(fin_all.at[at], r_fin.at[at])
                block = fin_all[at]
            else:
                block = fin[...]
            xx = m4(x + e)
            zz = zl if f == 0 else 1 - zl
            dw_v[:, pl.ds(pl.multiple_of(256 * xx + 128 * zz, 128), 128)] = block[0].astype(F32)
            dw_v[:, pl.ds(pl.multiple_of(1024 + 512 * zz + 128 * xx, 128), 128)] = block[1].astype(F32)
    last = pltpu.make_async_copy(dw_v, dw_hbm, dw_sem.at[0])
    last.start()

    for c in sent:
        c.wait_send()
    for h in range(HEADS):
        hc = pl.ds(h * HR, HR)
        for i, (src, dst) in enumerate(((q_v, dq_hbm), (k_v, dk_hbm), (v_v, dv_hbm))):
            pltpu.make_async_copy(src.at[:, hc], dst.at[:, hc], out_sem.at[i, h]).wait()
    last.wait()


def per_device(queries, keys, values, attn_out, out_grad, log_norm, segment_ids, kept_tokens, out_weight):
    hbm = pl.BlockSpec(memory_space=pl.ANY)
    dma = pltpu.SemaphoreType.DMA
    tok = jax.ShapeDtypeStruct((T, HW), BF16)
    V = pltpu.VMEM
    scratch = [
        V((T, HW), BF16), V((T, HW), BF16), V((T, HW), BF16),
        V((T, HW), BF16), V((SH, T, HR), BF16),
        V((2 * T, HW), BF16), V((SH * HR, 2 * T), BF16),
        V((SH, HR, HW), BF16), V((SH, HR, HW), BF16),
        V((HEADS, T, HR), BF16), V((SH, T, HR), BF16),
        V((T, T), F32), V((HEADS, T), F32),
        pltpu.SMEM((1, 4), jnp.int32), pltpu.SMEM((1, 4), jnp.int32),
        V((2, 4, HR, 256), BF16), V((2, 4, HR, 256), BF16), V((2, 4, 2, HR, 256), BF16),
        V((4, 2, HR, 256), BF16), V((3, 2, HR, 256), BF16), V((2, HR, 256), BF16), V((3, HR, HR), BF16),
        V((2, 4, 64, 512), BF16), V((2, 4, 64, 512), BF16), V((2, 4, HR, 512), BF16),
        V((4, HR, 512), BF16), V((3, HR, 512), BF16), V((HR, 512), BF16), V((3, HR, HR), BF16),
        V((2, HR, HR), BF16), V((8, 2, HR, HR), BF16), V((HR, HW), F32),
        dma((9,)), dma((3, HEADS)), dma((1,)),
        dma((17,)), dma((9,)), dma((8,)),
        dma((48,)), dma((1,)), dma((3, 2)), dma((2, 4, 2)), dma((2, 4, 2)),
        dma((24,)), dma((3,)), dma((2, 4)), dma((2, 4)),
        dma((72,)), dma((2, 4)), dma((2, 4, 2)), dma((3,)), dma((3,)),
        dma((2, 4)), dma((2, 4, 2)), dma((3,)), dma((3,)), dma((8,)),
    ]
    return pl.pallas_call(
        kernel,
        out_shape=(tok, tok, tok, jax.ShapeDtypeStruct((HR, HW), F32)),
        in_specs=[hbm] * 9,
        out_specs=(hbm,) * 4,
        scratch_shapes=scratch,
        compiler_params=pltpu.CompilerParams(
            collective_id=0, has_side_effects=True, vmem_limit_bytes=62 * 2**20
        ),
    )(queries, keys, values, attn_out, out_grad, log_norm.T, segment_ids, kept_tokens, out_weight)


def solution(mesh):
    token = P(("dp", "fsdp"), None)
    return jax.shard_map(
        per_device,
        mesh=mesh,
        in_specs=(token,) * 8 + (P("fsdp", None),),
        out_specs=(token, token, token, P("fsdp", None)),
        check_vma=False,
    )
```

time: 86.1 us -> 81.9 us (0.951)
  Pallas kernels: 75 us -> 72.4 us
  local copies, waits for them, and re-layouts: 10.2 us -> 8.59 us
    pallas_call x1, Pallas kernels: 75 us -> 72.4 us  [per_device(): pl.pallas_call(kernel, out_shape=(tok, tok, tok, jax.ShapeDtypeStruct((HR...]
    unnamed x11 -> x10, local copies, waits for them, and re-layouts: 10.2 us -> 8.59 us
where the time goes in v2:
time: 81.9 us; the launch traced here: 81.7 us
  Pallas kernels  72.4 us (88%)
  local copies, waits for them, and re-layouts  8.59 us (10%)
    pallas_call x1, Pallas kernels, per_device(): pl.pallas_call(kernel, out_shape=(tok, tok, tok, jax.ShapeDtypeStruct((HR...  72.4 us
    unnamed x10, local copies, waits for them, and re-layouts  8.59 us

profile of v2, /device:TPU:0, one launch (start us, length us, event | category | flops | bytes accessed | tf_op | source)
XLA Modules:
  0.0 81.7 jit_solution(17887885912938476790)
XLA Ops:
  0.6 72.4 %shard_map.120 = (bf16[512,2048]{1,0:T(8,128)(2,1)}, bf16[512,2048]{1,0:T(8,128)(2,1)}, bf16[512,2048]{1,0:T(8,128)(2,1)}, f32[128,2048]{1,0:T(8,128)}) custom-call(bf16[512,2048]{1,0:T(8,128)(2,1)} %q_hbm.1, bf16[512,2048]{1,0:T(8,128)(2,1)} %k_hbm.1, bf16[512,2048]{1,0:T(8,128)(2,1)} %v_hbm.1, bf16[512,2048]{1,0:T(8,128)(2,1)} %ao_hbm.1, ...), custom_call_target="tpu_custom_call" | custom-call | tf_op jit(solution)/shard_map/pallas_call | solution.py:501
  73.1 0.0 copy-start.1
  73.1 3.3 %copy.17 = bf16[512,2048]{1,0:T(8,128)(2,1)} copy(bf16[512,2048]{1,0:T(8,128)(2,1)} %get-tuple-element.8) | data formatting | bytes 4194304
  76.4 0.0 copy-done.1
  76.4 0.0 copy-start
  76.4 1.3 %copy.18 = bf16[512,2048]{1,0:T(8,128)(2,1)} copy(bf16[512,2048]{1,0:T(8,128)(2,1)S(1)} %copy-done.1) | data formatting | bytes 4194304
  77.7 1.0 %copy-done = bf16[512,2048]{1,0:T(8,128)(2,1)S(1)} copy-done((bf16[512,2048]{1,0:T(8,128)(2,1)S(1)}, bf16[512,2048]{1,0:T(8,128)(2,1)}, u32[]{:S(2)}) %copy-start) | copy-done | bytes 2097176
  78.7 0.0 copy-start.2
  78.7 1.3 %copy.19 = bf16[512,2048]{1,0:T(8,128)(2,1)} copy(bf16[512,2048]{1,0:T(8,128)(2,1)S(1)} %copy-done) | data formatting | bytes 4194304
  80.1 0.6 copy-done.2
  80.7 1.0 %copy.20 = f32[128,2048]{1,0:T(8,128)} copy(f32[128,2048]{1,0:T(8,128)S(1)} %copy-done.2) | data formatting | bytes 2097152
Async XLA Ops:
  73.1 3.3 %copy-start.1 = (bf16[512,2048]{1,0:T(8,128)(2,1)S(1)}, bf16[512,2048]{1,0:T(8,128)(2,1)}, u32[]{:S(2)}) copy-start(bf16[512,2048]{1,0:T(8,128)(2,1)} %get-tuple-element.9) | copy-start | bytes 6291460
  76.4 2.3 %copy-start = (bf16[512,2048]{1,0:T(8,128)(2,1)S(1)}, bf16[512,2048]{1,0:T(8,128)(2,1)}, u32[]{:S(2)}) copy-start(bf16[512,2048]{1,0:T(8,128)(2,1)} %get-tuple-element.10) | copy-start | bytes 6291460
  78.7 2.0 %copy-start.2 = (f32[128,2048]{1,0:T(8,128)S(1)}, f32[128,2048]{1,0:T(8,128)}, u32[]{:S(2)}) copy-start(f32[128,2048]{1,0:T(8,128)} %get-tuple-element.11) | copy-start | bytes 3145732

commit v3 on v2

--- a/solution.py
+++ b/solution.py
@@ -30,12 +30,12 @@
 
 def kernel(
     q_hbm, k_hbm, v_hbm, ao_hbm, og_hbm, ln_hbm, seg_hbm, kept_hbm, w_hbm,
-    dq_hbm, dk_hbm, dv_hbm, dw_hbm,
-    q_v, k_v, v_v, ao, po, g_all, aot, w_all, dwp, d_o, pg, bias, norm_t, seg_ref, kept_ref,
+    q_v, k_v, v_v, dw_v,
+    ao, po, g_all, aot, w_all, dwp, d_o, pg, bias, norm_t, seg_ref, kept_ref,
     ra, ta, sa, suma, ya, yra, za,
     rc, tc, sc, sumc, yc, yrc, xc,
-    fin, fin_all, dw_v,
-    load_sem, out_sem, dw_sem,
+    fin, fin_all,
+    load_sem,
     s_core, r_core, r_pg,
     s_a, r_a1, r_ay, r_ax, r_ax2,
     s_c, r_cy, r_cz, r_cz2,
@@ -141,18 +141,23 @@
         for e in es:
             send(part, part, "c", r_cy.at[(4 - e) - 1], at_y(e))
 
+    def a_piece(e, j, x_):
+        if e or j:
+            return row_k(e, j), cols_a(x_)
+        return k1, pl.ds(pl.multiple_of(1024 + x_ * 256, 128), 256)
+
     def a_to_x(e, j):
-        k = row_k(e, j)
-        part = w_all.at[k, :, ax]
+        k, c = a_piece(e, j, x)
+        part = w_all.at[k, :, c]
         send(part, part, "a", r_ax.at[0, e, j], at_x(1))
         send(part, part, "a", r_ax.at[1, e, j], at_x(3))
 
     def a_relay(e, j):
-        k = row_k(e, j)
-        lcol, rcol = cols_a(m4(x - 1)), cols_a(m4(x + 1))
+        k, lcol = a_piece(e, j, m4(x - 1))
         arrived(w_all.at[k, :, lcol], r_ax.at[0, e, j])
         part = w_all.at[k, pl.ds(0, 64), lcol]
         send(part, part, "a", r_ax2.at[0, e, j], at_x(1))
+        k, rcol = a_piece(e, j, m4(x + 1))
         arrived(w_all.at[k, :, rcol], r_ax.at[1, e, j])
         part = w_all.at[k, pl.ds(64, 64), rcol]
         send(part, part, "a", r_ax2.at[1, e, j], at_x(3))
@@ -185,14 +190,10 @@
         c_to_z(e)
 
     own_a = w_all.at[k0, :, ax]
-    own_c = w_all.at[k0, :, cz]
+    own_c = w_all.at[k0, :, pl.ds(pl.multiple_of(1024 + x * 256, 128), 256)]
     send(own_a, own_a, "a", r_a1.at[0], dev(x, y, zn, core))
-    a_to_y(k0, 0, (1, 3))
     c_to_y((1, 3))
-    a_to_y(k0, 0, (2,))
-    c_to_y((2,))
-    send(own_c, own_c, "c", r_cz.at[0, 0], dev(x, y, zn, core))
-    send(own_c, own_c, "c", r_cz.at[1, 0], at_z(2))
+    send(own_c, own_c, "a", r_a1.at[1], dev(x, y, zn, core))
 
     l_seg.wait()
     l_kept.wait()
@@ -217,40 +218,43 @@
     for i in range(SH):
         send(ao.at[:, head_cols(2 * i + 1 - core)], po.at[i], s_core.at[1 + i], r_core.at[1 + i], me_partner)
 
-    arrived(w_all.at[k1, :, ax], r_a1.at[0])
-    a_to_y(k1, 1, ORDER)
-    a_to_x(0, 1)
-
     def flip_own(lo, hi):
         for i in range(lo, hi):
             aot[pl.ds(i * HR, HR), pl.ds(0, T)] = jnp.transpose(ao[:, head_cols(2 * i + core)])
-
-    flip_own(0, 2)
-    a_step(1, 0)
-    a_step(3, 0)
-    flip_own(2, 4)
-    c_step(1)
-    c_step(3)
-    flip_own(4, 6)
-    a_step(2, 0)
-    c_step(2)
-    a_relay(0, 1)
-    flip_own(6, 8)
-    a_relay(1, 0)
-    a_relay(3, 0)
 
     def flip_other(lo, hi):
         for i in range(lo, hi):
             arrived(po.at[i], r_core.at[1 + i])
             aot[pl.ds(i * HR, HR), pl.ds(T, T)] = jnp.transpose(po[i])
 
+    arrived(w_all.at[k1, :, ax], r_a1.at[0])
+    a_to_x(0, 1)
+    k, c = a_piece(0, 0, x)
+    arrived(w_all.at[k, :, c], r_a1.at[1])
+    a_to_x(0, 0)
+    c_step(1)
+    c_step(3)
+    a_to_y(k0, 0, ORDER)
+    flip_own(0, 4)
+    a_relay(0, 1)
+    a_step(1, 0)
+    a_step(3, 0)
+    a_relay(0, 0)
+    a_step(2, 0)
+    c_to_y((2,))
+    a_to_y(k1, 1, ORDER)
+    flip_own(4, 8)
+    c_relay(1)
+    c_relay(3)
     arrived(g_all.at[pl.ds(T, T)], r_core.at[0])
     flip_other(0, 4)
-    c_relay(1)
-    c_relay(3)
+    a_relay(1, 0)
+    a_relay(3, 0)
+    flip_other(4, 8)
+    c_step(2)
+    a_relay(2, 0)
     a_step(1, 1)
     a_step(3, 1)
-    flip_other(4, 8)
     a_step(2, 1)
 
     def dw_group(e):
@@ -315,21 +319,14 @@
 
     dw_group(2)
     hop_far(2)
+    dw_group(1)
     hop_near(2)
-    a_relay(2, 0)
     c_relay(2)
-    dw_group(1)
-    hop_far(1)
-    hop_near(1)
     for e in ORDER:
         a_relay(e, 1)
+    hop_far(1)
     dw_group(3)
-    hop_far(3)
-    hop_near(3)
-    hop_relay(2)
     dw_group(0)
-    hop_far(0)
-    hop_near(0)
 
     for b in range(4):
         ok = lax.broadcasted_iota(jnp.int32, (128, 128), 0) < live[b]
@@ -339,20 +336,26 @@
     l_ln.wait()
     norm_t[...] = norm_t[...] * LOG2E
 
-    far_a = cols_a(x2)
+    hop_relay(2)
+    hop_near(1)
     for e in (0,) + ORDER:
         for j in (0, 1):
-            if e or j:
-                arrived(w_all.at[row_k(e, j), pl.ds(0, 64), far_a], r_ax2.at[0, e, j])
-                arrived(w_all.at[row_k(e, j), pl.ds(64, 64), far_a], r_ax2.at[1, e, j])
-    arrived(w_all.at[k1, :, cols_c(1 - zl)], r_cz.at[0, 0])
-    arrived(w_all.at[k1, :, cz], r_cz.at[1, 0])
+            k, c = a_piece(e, j, x2)
+            arrived(w_all.at[k, pl.ds(0, 64), c], r_ax2.at[0, e, j])
+            arrived(w_all.at[k, pl.ds(64, 64), c], r_ax2.at[1, e, j])
     for e in ORDER:
         k, c = z_place(2, e)
         arrived(w_all.at[k, pl.ds(0, 64), c], r_cz2.at[0, e])
         arrived(w_all.at[k, pl.ds(64, 64), c], r_cz2.at[1, e])
 
+    hop_far(3)
+
     for i in range(4):
+        if i == 2:
+            hop_relay(1)
+            hop_near(3)
+            hop_sum(2)
+            hop_far(0)
         wt = w_all[pl.ds(2 * i, 2)].reshape(2 * HR, HW)
         for part in (1, 0):
             got = dot_nt(g_all[pl.ds(part * T, T), :], wt).astype(BF16)
@@ -368,7 +371,6 @@
     l_q.wait()
     l_k.wait()
     l_v.wait()
-    hop_relay(1)
 
     def attention(parity, lo, hi):
         def body(i, carry):
@@ -388,28 +390,22 @@
             q_v[:, hc] = dq.astype(BF16)
             k_v[:, hc] = dk.astype(BF16)
             v_v[:, hc] = dv.astype(BF16)
-            pltpu.make_async_copy(q_v.at[:, hc], dq_hbm.at[:, hc], out_sem.at[0, h]).start()
-            pltpu.make_async_copy(k_v.at[:, hc], dk_hbm.at[:, hc], out_sem.at[1, h]).start()
-            pltpu.make_async_copy(v_v.at[:, hc], dv_hbm.at[:, hc], out_sem.at[2, h]).start()
             return carry
 
         lax.fori_loop(lo, hi, body, 0)
 
-    attention(core, 0, 1)
+    attention(core, 0, 2)
     hop_relay(3)
-    hop_sum(2)
-    attention(core, 1, 2)
+    hop_near(0)
+    hop_sum(1)
+    attention(core, 2, 6)
     hop_relay(0)
-    attention(core, 2, 4)
-    hop_sum(1)
-    attention(core, 4, 6)
     hop_sum(3)
     attention(core, 6, 8)
-    hop_sum(0)
-
     for i in range(SH):
         arrived(d_o.at[2 * i + 1 - core], r_pg.at[i])
     attention(1 - core, 0, 1)
+    hop_sum(0)
 
     tot = suma[0].astype(F32)
     totc = sumc[0].astype(F32)
@@ -429,7 +425,7 @@
         send(yra.at[lax.div(zz, 2), :, quarter(lax.rem(zz, 2))], za.at[(4 - e) - 1], "rs", r_za.at[(4 - e) - 1], at_z(e))
         send(yrc.at[:, quarter(m4(x + e))], xc.at[(4 - e) - 1], "rs", r_xc.at[(4 - e) - 1], at_x(e))
 
-    attention(1 - core, 1, 3)
+    attention(1 - core, 1, 4)
 
     for e in range(3):
         arrived(za.at[e], r_za.at[e])
@@ -447,7 +443,7 @@
                 at = ((4 - e) % 4) * 2 + f
                 send(fin, fin_all.at[at], "rs", r_fin.at[at], dev(m4(x + e), y, z if f == 0 else zs, core))
 
-    attention(1 - core, 3, 8)
+    attention(1 - core, 4, 8)
 
     for e in range(4):
         for f in (0, 1):
@@ -461,25 +457,25 @@
             zz = zl if f == 0 else 1 - zl
             dw_v[:, pl.ds(pl.multiple_of(256 * xx + 128 * zz, 128), 128)] = block[0].astype(F32)
             dw_v[:, pl.ds(pl.multiple_of(1024 + 512 * zz + 128 * xx, 128), 128)] = block[1].astype(F32)
-    last = pltpu.make_async_copy(dw_v, dw_hbm, dw_sem.at[0])
-    last.start()
 
     for c in sent:
         c.wait_send()
-    for h in range(HEADS):
-        hc = pl.ds(h * HR, HR)
-        for i, (src, dst) in enumerate(((q_v, dq_hbm), (k_v, dk_hbm), (v_v, dv_hbm))):
-            pltpu.make_async_copy(src.at[:, hc], dst.at[:, hc], out_sem.at[i, h]).wait()
-    last.wait()
+
+
+def to_hbm(q, k, v, w, dq, dk, dv, dw, sem):
+    copies = [pltpu.make_async_copy(a, b, sem.at[i]) for i, (a, b) in enumerate(((q, dq), (k, dk), (v, dv), (w, dw)))]
+    for c in copies:
+        c.start()
+    for c in copies:
+        c.wait()
 
 
 def per_device(queries, keys, values, attn_out, out_grad, log_norm, segment_ids, kept_tokens, out_weight):
     hbm = pl.BlockSpec(memory_space=pl.ANY)
     dma = pltpu.SemaphoreType.DMA
-    tok = jax.ShapeDtypeStruct((T, HW), BF16)
     V = pltpu.VMEM
+    tok = V((T, HW), BF16)
     scratch = [
-        V((T, HW), BF16), V((T, HW), BF16), V((T, HW), BF16),
         V((T, HW), BF16), V((SH, T, HR), BF16),
         V((2 * T, HW), BF16), V((SH * HR, 2 * T), BF16),
         V((SH, HR, HW), BF16), V((SH, HR, HW), BF16),
@@ -490,24 +486,32 @@
         V((4, 2, HR, 256), BF16), V((3, 2, HR, 256), BF16), V((2, HR, 256), BF16), V((3, HR, HR), BF16),
         V((2, 4, 64, 512), BF16), V((2, 4, 64, 512), BF16), V((2, 4, HR, 512), BF16),
         V((4, HR, 512), BF16), V((3, HR, 512), BF16), V((HR, 512), BF16), V((3, HR, HR), BF16),
-        V((2, HR, HR), BF16), V((8, 2, HR, HR), BF16), V((HR, HW), F32),
-        dma((9,)), dma((3, HEADS)), dma((1,)),
+        V((2, HR, HR), BF16), V((8, 2, HR, HR), BF16),
+        dma((9,)),
         dma((17,)), dma((9,)), dma((8,)),
-        dma((48,)), dma((1,)), dma((3, 2)), dma((2, 4, 2)), dma((2, 4, 2)),
+        dma((52,)), dma((2,)), dma((3, 2)), dma((2, 4, 2)), dma((2, 4, 2)),
         dma((24,)), dma((3,)), dma((2, 4)), dma((2, 4)),
         dma((72,)), dma((2, 4)), dma((2, 4, 2)), dma((3,)), dma((3,)),
         dma((2, 4)), dma((2, 4, 2)), dma((3,)), dma((3,)), dma((8,)),
     ]
-    return pl.pallas_call(
+    grads = pl.pallas_call(
         kernel,
-        out_shape=(tok, tok, tok, jax.ShapeDtypeStruct((HR, HW), F32)),
+        out_shape=(tok, tok, tok, V((HR, HW), F32)),
         in_specs=[hbm] * 9,
-        out_specs=(hbm,) * 4,
+        out_specs=(pl.BlockSpec(memory_space=pltpu.VMEM),) * 4,
         scratch_shapes=scratch,
         compiler_params=pltpu.CompilerParams(
-            collective_id=0, has_side_effects=True, vmem_limit_bytes=62 * 2**20
+            collective_id=0, has_side_effects=True, vmem_limit_bytes=48 * 2**20
         ),
     )(queries, keys, values, attn_out, out_grad, log_norm.T, segment_ids, kept_tokens, out_weight)
+    return pl.pallas_call(
+        to_hbm,
+        out_shape=tuple(jax.ShapeDtypeStruct(g.shape, g.dtype) for g in grads),
+        in_specs=[hbm] * 4,
+        out_specs=(hbm,) * 4,
+        scratch_shapes=[dma((4,))],
+        compiler_params=pltpu.CompilerParams(vmem_limit_bytes=2**20),
+    )(*grads)
 
 
 def solution(mesh):

time: 81.9 us -> 72.3 us (0.88)
  local copies, waits for them, and re-layouts: 8.59 us -> 0 us
  Pallas kernels: 72.4 us -> 71.4 us
    unnamed x10 -> x0, local copies, waits for them, and re-layouts: 8.59 us -> none
    pallas_call x1 -> x2, Pallas kernels: 72.4 us -> 71.4 us  [the longest x1 68.4 us: per_device(): pl.pallas_call(kernel, out_shape=(tok, tok, tok, V((HR, HW), F32)), in_sp...]
where the time goes in v3:
time: 72.3 us; the launch traced here: 72 us
  Pallas kernels  71.4 us (99%)
    pallas_call x1, Pallas kernels, per_device(): pl.pallas_call(kernel, out_shape=(tok, tok, tok, V((HR, HW), F32)), in_sp...  68.4 us
    pallas_call x1, Pallas kernels, per_device(): pl.pallas_call(to_hbm, out_shape=tuple((jax.ShapeDtypeStruct(g.shape, g.d...  3.02 us

profile of v3, /device:TPU:0, one launch (start us, length us, event | category | flops | bytes accessed | tf_op | source)
XLA Modules:
  0.0 72.0 jit_solution(5930817767795367232)
XLA Ops:
  0.6 68.4 %shard_map.120 = (bf16[512,2048]{1,0:T(8,128)(2,1)S(1)}, bf16[512,2048]{1,0:T(8,128)(2,1)S(1)}, bf16[512,2048]{1,0:T(8,128)(2,1)S(1)}, f32[128,2048]{1,0:T(8,128)S(1)}) custom-call(bf16[512,2048]{1,0:T(8,128)(2,1)} %q_hbm.1, bf16[512,2048]{1,0:T(8,128)(2,1)} %k_hbm.1, bf16[512,2048]{1,0:T(8,128)(2,1)} %v_hbm.1, bf16[512,2048]{1,0:T(8,128)(2,1)} %ao_hbm.1, ...), custom_call_target="tpu_custom_call" | custom-call | tf_op jit(solution)/shard_map/pallas_call | solution.py:497
  69.0 3.0 %shard_map.121 = (bf16[512,2048]{1,0:T(8,128)(2,1)}, bf16[512,2048]{1,0:T(8,128)(2,1)}, bf16[512,2048]{1,0:T(8,128)(2,1)}, f32[128,2048]{1,0:T(8,128)}) custom-call(bf16[512,2048]{1,0:T(8,128)(2,1)S(1)} %get-tuple-element.8.q, bf16[512,2048]{1,0:T(8,128)(2,1)S(1)} %get-tuple-element.9.k, bf16[512,2048]{1,0:T(8,128)(2,1)S(1)} %get-tuple-element.10.v, ...), custom_call_target="tpu_custom_call" | custom-call | tf_op jit(solution)/shard_map/pallas_call | solution.py:507

commit v4 on v3

--- a/solution.py
+++ b/solution.py
@@ -142,9 +142,7 @@
             send(part, part, "c", r_cy.at[(4 - e) - 1], at_y(e))
 
     def a_piece(e, j, x_):
-        if e or j:
-            return row_k(e, j), cols_a(x_)
-        return k1, pl.ds(pl.multiple_of(1024 + x_ * 256, 128), 256)
+        return row_k(e, j), cols_a(x_)
 
     def a_to_x(e, j):
         k, c = a_piece(e, j, x)
@@ -190,10 +188,8 @@
         c_to_z(e)
 
     own_a = w_all.at[k0, :, ax]
-    own_c = w_all.at[k0, :, pl.ds(pl.multiple_of(1024 + x * 256, 128), 256)]
     send(own_a, own_a, "a", r_a1.at[0], dev(x, y, zn, core))
     c_to_y((1, 3))
-    send(own_c, own_c, "a", r_a1.at[1], dev(x, y, zn, core))
 
     l_seg.wait()
     l_kept.wait()
@@ -218,6 +214,9 @@
     for i in range(SH):
         send(ao.at[:, head_cols(2 * i + 1 - core)], po.at[i], s_core.at[1 + i], r_core.at[1 + i], me_partner)
 
+    part = w_all.at[k0, :, cols_c(1 - zl)]
+    send(part, part, "c", r_cz.at[0, 0], dev(x, y, zn, core))
+
     def flip_own(lo, hi):
         for i in range(lo, hi):
             aot[pl.ds(i * HR, HR), pl.ds(0, T)] = jnp.transpose(ao[:, head_cols(2 * i + core)])
@@ -229,9 +228,6 @@
 
     arrived(w_all.at[k1, :, ax], r_a1.at[0])
     a_to_x(0, 1)
-    k, c = a_piece(0, 0, x)
-    arrived(w_all.at[k, :, c], r_a1.at[1])
-    a_to_x(0, 0)
     c_step(1)
     c_step(3)
     a_to_y(k0, 0, ORDER)
@@ -239,8 +235,10 @@
     a_relay(0, 1)
     a_step(1, 0)
     a_step(3, 0)
-    a_relay(0, 0)
     a_step(2, 0)
+    part = w_all.at[k1, :, cz]
+    arrived(part, r_cz.at[0, 0])
+    send(part, part, "c", r_cz.at[1, 0], dev(x, y, zs, core))
     c_to_y((2,))
     a_to_y(k1, 1, ORDER)
     flip_own(4, 8)
@@ -300,7 +298,7 @@
             tc[d, e] = (dwp[k, part, c].astype(F32) + rc[d, e].astype(F32)).astype(BF16)
             send(tc.at[d, e], sc.at[d, e, part], "rs", r_sc.at[d, e, d], to_z)
 
-    def hop_sum(e):
+    def hop_sum_a(e):
         for d in (0, 1):
             for f in (0, 1):
                 arrived(sa.at[d, e, f], r_sa.at[d, e, f])
@@ -308,6 +306,8 @@
         suma[e] = (own.astype(F32) + sa[0, e].astype(F32) + sa[1, e].astype(F32)).astype(BF16)
         if e:
             send(suma.at[e], ya.at[(4 - e) - 1], "rs", r_ya.at[(4 - e) - 1], at_y(e))
+
+    def hop_sum_c(e):
         for d in (0, 1):
             for f in (0, 1):
                 part = top if f == 0 else low
@@ -316,6 +316,10 @@
         sumc[e] = (own.astype(F32) + sc[0, e].astype(F32) + sc[1, e].astype(F32)).astype(BF16)
         if e:
             send(sumc.at[e], yc.at[(4 - e) - 1], "rs", r_yc.at[(4 - e) - 1], at_y(e))
+
+    def hop_sum(e):
+        hop_sum_a(e)
+        hop_sum_c(e)
 
     dw_group(2)
     hop_far(2)
@@ -340,9 +344,11 @@
     hop_near(1)
     for e in (0,) + ORDER:
         for j in (0, 1):
-            k, c = a_piece(e, j, x2)
-            arrived(w_all.at[k, pl.ds(0, 64), c], r_ax2.at[0, e, j])
-            arrived(w_all.at[k, pl.ds(64, 64), c], r_ax2.at[1, e, j])
+            if e or j:
+                k, c = a_piece(e, j, x2)
+                arrived(w_all.at[k, pl.ds(0, 64), c], r_ax2.at[0, e, j])
+                arrived(w_all.at[k, pl.ds(64, 64), c], r_ax2.at[1, e, j])
+    arrived(w_all.at[k1, :, cols_c(1 - zl)], r_cz.at[1, 0])
     for e in ORDER:
         k, c = z_place(2, e)
         arrived(w_all.at[k, pl.ds(0, 64), c], r_cz2.at[0, e])
@@ -405,51 +411,53 @@
     for i in range(SH):
         arrived(d_o.at[2 * i + 1 - core], r_pg.at[i])
     attention(1 - core, 0, 1)
-    hop_sum(0)
-
+    def quarter(i):
+        return pl.ds(pl.multiple_of(i * HR, HR), HR)
+
+    hop_sum_a(0)
     tot = suma[0].astype(F32)
-    totc = sumc[0].astype(F32)
     for e in (2, 1, 3):
         arrived(ya.at[e - 1], r_ya.at[e - 1])
         tot = tot + ya[e - 1].astype(F32)
-        arrived(yc.at[e - 1], r_yc.at[e - 1])
-        totc = totc + yc[e - 1].astype(F32)
     yra[...] = tot.astype(BF16)
-    yrc[...] = totc.astype(BF16)
-
-    def quarter(i):
-        return pl.ds(pl.multiple_of(i * HR, HR), HR)
-
-    for e in (1, 3, 2):
+    for e in (2, 1, 3):
         zz = m4(z + e)
         send(yra.at[lax.div(zz, 2), :, quarter(lax.rem(zz, 2))], za.at[(4 - e) - 1], "rs", r_za.at[(4 - e) - 1], at_z(e))
+    hop_sum_c(0)
+    tot = sumc[0].astype(F32)
+    for e in (2, 1, 3):
+        arrived(yc.at[e - 1], r_yc.at[e - 1])
+        tot = tot + yc[e - 1].astype(F32)
+    yrc[...] = tot.astype(BF16)
+    for e in (2, 1, 3):
         send(yrc.at[:, quarter(m4(x + e))], xc.at[(4 - e) - 1], "rs", r_xc.at[(4 - e) - 1], at_x(e))
 
-    attention(1 - core, 1, 4)
-
-    for e in range(3):
-        arrived(za.at[e], r_za.at[e])
-        arrived(xc.at[e], r_xc.at[e])
-    tot = yra[zh, :, quarter(zl)].astype(F32)
-    totc = yrc[:, quarter(x)].astype(F32)
-    for e in range(3):
-        tot = tot + za[e].astype(F32)
-        totc = totc + xc[e].astype(F32)
-    fin[0] = tot.astype(BF16)
-    fin[1] = totc.astype(BF16)
-    for e in range(4):
-        for f in (0, 1):
-            if e or f:
-                at = ((4 - e) % 4) * 2 + f
-                send(fin, fin_all.at[at], "rs", r_fin.at[at], dev(m4(x + e), y, z if f == 0 else zs, core))
-
-    attention(1 - core, 4, 8)
+    attention(1 - core, 1, 3)
+
+    def finished(n, own, parts, sems):
+        tot = own.astype(F32)
+        for e in range(3):
+            arrived(parts.at[e], sems.at[e])
+            tot = tot + parts[e].astype(F32)
+        fin[n] = tot.astype(BF16)
+        for e in (2, 1, 3, 0):
+            for f in (1, 0):
+                if e or f:
+                    at = ((4 - e) % 4) * 2 + f
+                    to = dev(m4(x + e), y, z if f == 0 else zs, core)
+                    send(fin.at[n], fin_all.at[at, n], "rs", r_fin.at[at, n], to)
+
+    finished(0, yra[zh, :, quarter(zl)], za, r_za)
+    finished(1, yrc[:, quarter(x)], xc, r_xc)
+
+    attention(1 - core, 3, 8)
 
     for e in range(4):
         for f in (0, 1):
             at = e * 2 + f
             if at:
-                arrived(fin_all.at[at], r_fin.at[at])
+                arrived(fin_all.at[at, 0], r_fin.at[at, 0])
+                arrived(fin_all.at[at, 1], r_fin.at[at, 1])
                 block = fin_all[at]
             else:
                 block = fin[...]
@@ -489,10 +497,10 @@
         V((2, HR, HR), BF16), V((8, 2, HR, HR), BF16),
         dma((9,)),
         dma((17,)), dma((9,)), dma((8,)),
-        dma((52,)), dma((2,)), dma((3, 2)), dma((2, 4, 2)), dma((2, 4, 2)),
+        dma((48,)), dma((1,)), dma((3, 2)), dma((2, 4, 2)), dma((2, 4, 2)),
         dma((24,)), dma((3,)), dma((2, 4)), dma((2, 4)),
-        dma((72,)), dma((2, 4)), dma((2, 4, 2)), dma((3,)), dma((3,)),
-        dma((2, 4)), dma((2, 4, 2)), dma((3,)), dma((3,)), dma((8,)),
+        dma((80,)), dma((2, 4)), dma((2, 4, 2)), dma((3,)), dma((3,)),
+        dma((2, 4)), dma((2, 4, 2)), dma((3,)), dma((3,)), dma((8, 2)),
     ]
     grads = pl.pallas_call(
         kernel,

time: 72.3 us -> 70.2 us (0.971)
  Pallas kernels: 71.4 us -> 69.5 us
    pallas_call x1, Pallas kernels: 68.4 us -> 66.5 us  [per_device(): pl.pallas_call(kernel, out_shape=(tok, tok, tok, V((HR, HW), F32)), in_sp...]
where the time goes in v4:
time: 70.2 us; the launch traced here: 70.1 us
  Pallas kernels  69.5 us (99%)
    pallas_call x1, Pallas kernels, per_device(): pl.pallas_call(kernel, out_shape=(tok, tok, tok, V((HR, HW), F32)), in_sp...  66.5 us
    pallas_call x1, Pallas kernels, per_device(): pl.pallas_call(to_hbm, out_shape=tuple((jax.ShapeDtypeStruct(g.shape, g.d...  3.02 us

profile of v4, /device:TPU:0, one launch (start us, length us, event | category | flops | bytes accessed | tf_op | source)
XLA Modules:
  0.0 70.1 jit_solution(3653543592809655633)
XLA Ops:
  0.6 66.5 %shard_map.120 = (bf16[512,2048]{1,0:T(8,128)(2,1)S(1)}, bf16[512,2048]{1,0:T(8,128)(2,1)S(1)}, bf16[512,2048]{1,0:T(8,128)(2,1)S(1)}, f32[128,2048]{1,0:T(8,128)S(1)}) custom-call(bf16[512,2048]{1,0:T(8,128)(2,1)} %q_hbm.1, bf16[512,2048]{1,0:T(8,128)(2,1)} %k_hbm.1, bf16[512,2048]{1,0:T(8,128)(2,1)} %v_hbm.1, bf16[512,2048]{1,0:T(8,128)(2,1)} %ao_hbm.1, ...), custom_call_target="tpu_custom_call" | custom-call | tf_op jit(solution)/shard_map/pallas_call | solution.py:505
  67.1 3.0 %shard_map.121 = (bf16[512,2048]{1,0:T(8,128)(2,1)}, bf16[512,2048]{1,0:T(8,128)(2,1)}, bf16[512,2048]{1,0:T(8,128)(2,1)}, f32[128,2048]{1,0:T(8,128)}) custom-call(bf16[512,2048]{1,0:T(8,128)(2,1)S(1)} %get-tuple-element.8.q, bf16[512,2048]{1,0:T(8,128)(2,1)S(1)} %get-tuple-element.9.k, bf16[512,2048]{1,0:T(8,128)(2,1)S(1)} %get-tuple-element.10.v, ...), custom_call_target="tpu_custom_call" | custom-call | tf_op jit(solution)/shard_map/pallas_call | solution.py:515

commit v5 on v4

--- a/solution.py
+++ b/solution.py
@@ -400,17 +400,16 @@
 
         lax.fori_loop(lo, hi, body, 0)
 
-    attention(core, 0, 2)
+    attention(core, 0, 1)
     hop_relay(3)
     hop_near(0)
     hop_sum(1)
-    attention(core, 2, 6)
+    attention(core, 1, 4)
     hop_relay(0)
     hop_sum(3)
-    attention(core, 6, 8)
+    attention(core, 4, 8)
     for i in range(SH):
         arrived(d_o.at[2 * i + 1 - core], r_pg.at[i])
-    attention(1 - core, 0, 1)
     def quarter(i):
         return pl.ds(pl.multiple_of(i * HR, HR), HR)
 
@@ -432,7 +431,7 @@
     for e in (2, 1, 3):
         send(yrc.at[:, quarter(m4(x + e))], xc.at[(4 - e) - 1], "rs", r_xc.at[(4 - e) - 1], at_x(e))
 
-    attention(1 - core, 1, 3)
+    attention(1 - core, 0, 2)
 
     def finished(n, own, parts, sems):
         tot = own.astype(F32)
@@ -450,7 +449,7 @@
     finished(0, yra[zh, :, quarter(zl)], za, r_za)
     finished(1, yrc[:, quarter(x)], xc, r_xc)
 
-    attention(1 - core, 3, 8)
+    attention(1 - core, 2, 8)
 
     for e in range(4):
         for f in (0, 1):

time: 70.2 us -> 69.5 us (0.990)
  no operation moved by 1% of the time
where the time goes in v5:
time: 69.5 us; the launch traced here: 69.4 us
  Pallas kernels  68.8 us (99%)
    pallas_call x1, Pallas kernels, per_device(): pl.pallas_call(kernel, out_shape=(tok, tok, tok, V((HR, HW), F32)), in_sp...  65.8 us
    pallas_call x1, Pallas kernels, per_device(): pl.pallas_call(to_hbm, out_shape=tuple((jax.ShapeDtypeStruct(g.shape, g.d...  3.02 us

profile of v5, /device:TPU:0, one launch (start us, length us, event | category | flops | bytes accessed | tf_op | source)
XLA Modules:
  0.0 69.4 jit_solution(7618142885617939749)
XLA Ops:
  0.6 65.8 %shard_map.120 = (bf16[512,2048]{1,0:T(8,128)(2,1)S(1)}, bf16[512,2048]{1,0:T(8,128)(2,1)S(1)}, bf16[512,2048]{1,0:T(8,128)(2,1)S(1)}, f32[128,2048]{1,0:T(8,128)S(1)}) custom-call(bf16[512,2048]{1,0:T(8,128)(2,1)} %q_hbm.1, bf16[512,2048]{1,0:T(8,128)(2,1)} %k_hbm.1, bf16[512,2048]{1,0:T(8,128)(2,1)} %v_hbm.1, bf16[512,2048]{1,0:T(8,128)(2,1)} %ao_hbm.1, ...), custom_call_target="tpu_custom_call" | custom-call | tf_op jit(solution)/shard_map/pallas_call | solution.py:504
  66.4 3.0 %shard_map.121 = (bf16[512,2048]{1,0:T(8,128)(2,1)}, bf16[512,2048]{1,0:T(8,128)(2,1)}, bf16[512,2048]{1,0:T(8,128)(2,1)}, f32[128,2048]{1,0:T(8,128)}) custom-call(bf16[512,2048]{1,0:T(8,128)(2,1)S(1)} %get-tuple-element.8.q, bf16[512,2048]{1,0:T(8,128)(2,1)S(1)} %get-tuple-element.9.k, bf16[512,2048]{1,0:T(8,128)(2,1)S(1)} %get-tuple-element.10.v, ...), custom_call_target="tpu_custom_call" | custom-call | tf_op jit(solution)/shard_map/pallas_call | solution.py:514
